TPU v7x, 256 devices: a whole 4x4x8 slice. The times are simulated.
256 devices in a mesh: row: 16 (over x_lo, y, core), col: 16 (over z, x_hi).
Axes of the slice: x: 4 (x_hi: 2, x_lo: 2; x = x_hi * 2 + x_lo), y: 4, z: 8, core: 2. Of those that a mesh axis runs over, the one named last changes fastest.
Arguments:
- amplitudes: bfloat16 [6144, 163840], P('row', 'col'), may hold values from -6 to 6
- integrals: bfloat16 [163840, 1024], P('col', 'row'), may hold values from -0.01953125 to 0.01953125
- pair_first: int32 [1024], P('col'), may hold values from 0 to 1599
- pair_second: int32 [1024], P('col'), may hold values from 0 to 1599
- occ_energy: float32 [200], replicated, may hold values from -1 to -0.5
- vir_energy: float32 [1600], replicated, may hold values from 0.25 to 1
Outputs:
- update: bfloat16 [6144, 1024], P('row', 'col')
All inputs are finite; a program needn't handle non-finite values.
Results may differ from a plain program's by a relative error of at most 0.001.
Values may be sent and summed in bfloat16 or wider, within the bound.
No kernel may reach another device: no remote copies, remote signals or barrier semaphores. Data moves between devices by JAX's collectives and lax.ppermute only.
A program may use at most 128 MiB of HBM per device.

v0:
```python
import jax
import jax.numpy as jnp
from jax import lax
from jax.sharding import PartitionSpec as P


def lookup(indices, table):
    places = jnp.arange(table.shape[0], dtype=jnp.int32)
    return jnp.sum(jnp.where(indices[:, None] == places[None, :], table[None, :], 0.0), axis=1)


def on_device(amplitudes, integrals, pair_first, pair_second, occ_energy, vir_energy):
    local_rows = amplitudes.shape[0]
    partial_value = jnp.dot(
        amplitudes,
        lax.all_gather(integrals, "row", axis=1, tiled=True),
        preferred_element_type=jnp.float32,
    )
    ladder = lax.psum_scatter(partial_value, "col", scatter_dimension=1, tiled=True)
    nocc_count = occ_energy.shape[0]
    pair_rows = lax.axis_index("row") * local_rows + jnp.arange(local_rows, dtype=jnp.int32)
    first_occ = lookup(pair_rows // nocc_count, occ_energy)
    second_occ = lookup(pair_rows % nocc_count, occ_energy)
    first_vir = lookup(pair_first, vir_energy)
    second_vir = lookup(pair_second, vir_energy)
    denominator = (
        first_occ[:, None] + second_occ[:, None] - first_vir[None, :] - second_vir[None, :]
    )
    return (ladder / denominator).astype(jnp.bfloat16)


def solution(mesh):
    placed = (P("row", "col"), P("col", "row"), P("col"), P("col"), P(), P())
    return jax.shard_map(
        on_device, mesh=mesh, in_specs=placed, out_specs=P("row", "col"), check_vma=False
    )
```

profile of v0, /device:TPU:1, one launch (start us, length us, event | category | flops | bytes accessed | tf_op | source)
XLA Modules:
  0.0 354.1 jit_solution(2498226233036772760)
XLA Ops:
  6.5 0.0 all-gather.2.cloned.1.call-start
  6.5 0.7 all-gather.2.cloned.1.call-update
  7.3 0.0 copy-start.1
  7.3 0.0 copy-start
  7.3 0.0 copy-start.2
  7.3 0.0 copy-start.3
  7.3 0.0 reduce-scatter.2.cloned.1.call-start
  7.3 120.0 %all-gather.2.cloned.1.call-done = bf16[10240,1024]{0,1:T(8,128)(2,1)} async-done(((bf16[10240,64]{0,1:T(8,128)(2,1)}), bf16[10240,1024]{0,1:T(8,128)(2,1)}) %all-gather.2.cloned.1.call-update) | async-done | bytes 20971536 | tf_op jit(solution)/shard_map/all_gather | solution.py:16
  127.4 17.5 %fusion.5 = f32[384,1024]{0,1:T(8,128)} fusion(bf16[384,10240]{1,0:T(8,128)(2,1)} %param.6, bf16[10240,1024]{0,1:T(8,128)(2,1)} %all-gather.2.cloned.1.call-done), kind=kOutput, calls=%fused_computation.18 | convolution fusion | flops 8053063680 | bytes 30408704 | tf_op jit(solution)/shard_map/dot_general | solution.py:14
  144.9 0.0 reduce-scatter.2.cloned.1.call-update
  145.0 0.0 copy-done.1
  145.0 0.2 select_reduce_fusion.2
  145.1 0.0 copy-done
  145.2 0.0 copy-done.2
  145.2 0.0 copy-done.3
  145.2 0.3 select_reduce_fusion.1
  145.4 200.3 %reduce-scatter.2.cloned.1.call-done = f32[384,64]{0,1:T(8,128)} async-done(((f32[384,1024]{0,1:T(8,128)}), f32[384,64]{0,1:T(8,128)}) %reduce-scatter.2.cloned.1.call-update) | async-done | bytes 98320 | tf_op jit(solution)/shard_map/reduce_scatter | solution.py:19
  345.7 1.6 divide_convert_fusion
  (2 shorter events, 0.0 us)
Async XLA Ops:
  6.5 120.8 %all-gather.2.cloned.1.call-start = ((), (), s32[]{:S(2)}) async-start(), calls=%async_computation.1 | async-start | bytes 22282240 | tf_op jit(solution)/shard_map/all_gather | solution.py:16
  7.3 137.7 %copy-start.1 = (f32[200]{0:T(256)S(1)}, f32[200]{0:T(256)}, u32[]{:S(2)}) copy-start(f32[200]{0:T(256)} %param.10) | copy-start | bytes 2404
  7.3 137.9 %copy-start = (f32[1600]{0:T(1024)S(1)}, f32[1600]{0:T(1024)}, u32[]{:S(2)}) copy-start(f32[1600]{0:T(1024)} %param.11) | copy-start | bytes 19204
  7.3 137.9 %copy-start.2 = (s32[64]{0:T(128)S(1)}, s32[64]{0:T(128)}, u32[]{:S(2)}) copy-start(s32[64]{0:T(128)} %param.8) | copy-start | bytes 772
  7.3 137.9 %copy-start.3 = (s32[64]{0:T(128)S(1)}, s32[64]{0:T(128)}, u32[]{:S(2)}) copy-start(s32[64]{0:T(128)} %param.9) | copy-start | bytes 772
  7.3 338.4 %reduce-scatter.2.cloned.1.call-start = ((), (), s32[]{:S(2)}) async-start(), calls=%async_computation.2 | async-start | bytes 1671168 | tf_op jit(solution)/shard_map/reduce_scatter | solution.py:19
Sparse Core Ops, SparseCore 0:
  9.2 118.1 all-gather.1
  145.1 200.5 reduce-scatter.1
where the time goes:
time: 358 us; the launch traced here: 354 us
  waiting for transfers between devices  321 us (90%)
  matrix products  17.5 us (5%)
  between operations  13.5 us (4%)
    reduce_scatter x1, waiting for transfers between devices, on_device(): lax.psum_scatter(partial_value, 'col', scatter_dimension=1, tiled=True)  200 us
    all_gather x1, waiting for transfers between devices, on_device(): lax.all_gather(integrals, 'row', axis=1, tiled=True)  120 us
    dot_general x1, matrix products, on_device(): jnp.dot(amplitudes, lax.all_gather(integrals, 'row', axis=1, tiled=True),...  17.5 us
  transfers between devices with their start and end apart: 2, of which 2 were waited for; matrix products, arithmetic and copies ran while one was open for 0% of the time, Pallas kernels for 0%

commit v1 on v0

v1 whole, which is shorter than its diff:
```python
import functools

import jax
import jax.numpy as jnp
from jax import lax
from jax.experimental import pallas as pl
from jax.experimental.pallas import tpu as pltpu
from jax.sharding import PartitionSpec as P

YS, ZS = 4, 8
STEP = {"x": (1, 0), "U": (0, 1), "D": (0, -1)}
SLICES = ((64, (0, 0, 0, 1, 1, 2, 4), "DUxxDxD", "xUDUDUU"),)
DEPTH = 2048
GROUPS = (((0, 4), (4, 7), (7, 8)),)
ORDER = (
    ("s00", ()), ("s01", ()), ("s02", ()), ("s03", ("own",)), ("s04", ("s00",)), ("s05", ("s01",)),
    ("m00", ()), ("s06", ("m00",)), ("m01", ()), ("m02", ("m01",)),
)


def places(sources, ways):
    at = [(0, 0)]
    for source, way in zip(sources, ways):
        dx, dy = at[source]
        at.append((dx ^ STEP[way][0], (dy + STEP[way][1]) % YS))
    return at


def row_perm(ways):
    return [
        ((x * YS + y) * 2 + c, ((x ^ STEP[w][0]) * YS + (y + STEP[w][1]) % YS) * 2 + c)
        for x in range(2)
        for y in range(YS)
        for c, w in enumerate(ways)
    ]


PARTNER = [(r, r ^ 1) for r in range(4 * YS)]


def swap_perm(flip):
    pairs = []
    for xy in range(2 * YS):
        for c in range(2):
            for z in range(ZS):
                for h in range(2):
                    pairs.append((((xy * 2 + c) * ZS + z) * 2 + h, ((xy * 2 + (h ^ flip)) * ZS + z) * 2 + c))
    return pairs


def lookup(indices, table):
    places = jnp.arange(table.shape[0], dtype=jnp.int32)
    return jnp.sum(jnp.where(indices[:, None] == places[None, :], table[None, :], 0.0), axis=1)


def turn_kernel(rows, out):
    out[...] = rows[...].T


def turned(amplitudes):
    rows, depth = amplitudes.shape
    return pl.pallas_call(
        turn_kernel,
        grid=(depth // DEPTH,),
        in_specs=[pl.BlockSpec((rows, DEPTH), lambda k: (0, k))],
        out_specs=pl.BlockSpec((DEPTH, rows), lambda k: (k, 0)),
        out_shape=jax.ShapeDtypeStruct((depth, rows), amplitudes.dtype),
        cost_estimate=pl.CostEstimate(flops=0, bytes_accessed=0, transcendentals=0),
    )(amplitudes)


def accumulate(total, blocks, amplitudes):
    step = pl.program_id(0)
    stacked = jnp.concatenate([block[...] for block in blocks], axis=0)
    for half, rows in enumerate(amplitudes):
        count = rows.shape[1]
        columns = slice(half * count, (half + 1) * count)
        part = jnp.dot(stacked, rows[...], preferred_element_type=jnp.float32)

        @pl.when(step == 0)
        def _():
            total[:, columns] = part

        @pl.when(step > 0)
        def _():
            total[:, columns] += part


def product_kernel(*refs):
    *blocks, own, other, total = refs
    accumulate(total, blocks, (own, other))


def finish_kernel(counts, spots, *refs):
    last = counts[-1]
    blocks, (own, other) = refs[:last], refs[last : last + 2]
    earlier, out, total = refs[last + 2 : -2], refs[-2], refs[-1]
    accumulate(total, blocks, (own, other))

    @pl.when(pl.program_id(0) == pl.num_programs(0) - 1)
    def _():
        row = lax.axis_index("row")
        x, y, core = row // (2 * YS), row // 2 % YS, row % 2
        n = out.shape[1]
        i = 0
        for count, sums in zip(counts, (*earlier, total)):
            for j in range(count):
                (x0, y0), (x1, y1) = spots[0][i], spots[1][i]
                from_x = jnp.where(core == 0, x ^ x0, x ^ x1)
                from_y = jnp.where(core == 0, (y + YS - y0) % YS, (y + YS - y1) % YS)
                out[from_x * YS + from_y] = sums[j * n : (j + 1) * n, :]
                i += 1


def multiply(kernel, blocks, own, other, earlier, out_shape, scratch):
    n, depth = blocks[0].shape
    rows = own.shape[1]
    whole = lambda shape: pl.BlockSpec(shape, lambda k: (0,) * len(shape))
    return pl.pallas_call(
        kernel,
        grid=(depth // DEPTH,),
        in_specs=[pl.BlockSpec((n, DEPTH), lambda k: (0, k))] * len(blocks)
        + [pl.BlockSpec((DEPTH, rows), lambda k: (k, 0))] * 2
        + [whole(sums.shape) for sums in earlier],
        out_specs=whole(out_shape),
        out_shape=jax.ShapeDtypeStruct(out_shape, jnp.float32),
        scratch_shapes=scratch,
        compiler_params=pltpu.CompilerParams(vmem_limit_bytes=16 * 1024 * 1024),
        cost_estimate=pl.CostEstimate(flops=0, bytes_accessed=0, transcendentals=0),
    )(*blocks, own, other, *earlier)


def sums_of(blocks, own, other):
    n, width = blocks[0].shape[0], 2 * own.shape[1]
    return multiply(product_kernel, blocks, own, other, (), (len(blocks) * n, width), ())


def last_sums(blocks, own, other, earlier, spots, groups):
    n, width = blocks[0].shape[0], 2 * own.shape[1]
    counts = tuple(b - a for a, b in groups)
    kernel = functools.partial(finish_kernel, counts, spots)
    scratch = [pltpu.VMEM((len(blocks) * n, width), jnp.float32)]
    return multiply(kernel, blocks, own, other, earlier, (8, n, width), scratch)


def after(value, *others):
    return lax.optimization_barrier((value, *others))[0]


def partials(rows, amplitudes):
    done = {"other": turned(lax.ppermute(amplitudes, "row", PARTNER)), "own": turned(amplitudes)}
    held, earlier, start = [], [], 0
    for n, *_ in SLICES:
        held.append([lax.slice_in_dim(rows, start, start + n, axis=0)])
        earlier.append([])
        start += n
    for name, needs in ORDER:
        s, i = int(name[1]), int(name[2])
        n, sources, first, second = SLICES[s]
        if name[0] == "s":
            block = after(held[s][sources[i]], *(done[need] for need in needs))
            done[name] = lax.ppermute(block, "row", row_perm((first[i], second[i])))
            held[s].append(done[name])
            continue
        a, b = GROUPS[s][i]
        blocks = held[s][a:b]
        blocks[0] = after(blocks[0], *(done[need] for need in needs))
        if b < 8:
            done[name] = sums_of(blocks, done["own"], done["other"])
            earlier[s].append(done[name])
        else:
            spots = (places(sources, first), places(sources, second))
            done[name] = last_sums(blocks, done["own"], done["other"], earlier[s], spots, GROUPS[s])
            yield done[name]


def on_device(amplitudes, integrals, pair_first, pair_second, occ_energy, vir_energy):
    local_rows = amplitudes.shape[0]
    row, col = lax.axis_index("row"), lax.axis_index("col")
    core, h = row % 2, col % 2
    same = h == core
    along_z = [[z * 2 + b for z in range(ZS)] for b in range(2)]
    done = []
    for sums in partials(integrals.T, amplitudes):
        if done:
            sums = after(sums, shares)
        shares = lax.all_to_all(sums, "col", split_axis=0, concat_axis=0, tiled=True, axis_index_groups=along_z)
        mine = jnp.sum(shares, axis=0)
        own, theirs = mine[:, :local_rows], mine[:, local_rows:]
        a = lax.ppermute(jnp.where(same, own, theirs), ("row", "col"), swap_perm(0))
        b = lax.ppermute(jnp.where(same, theirs, own), ("row", "col"), swap_perm(1))
        done.append(a + b)
    ladder = jnp.concatenate(done, axis=0)

    nocc_count = occ_energy.shape[0]
    pair_rows = row * local_rows + jnp.arange(local_rows, dtype=jnp.int32)
    first_occ = lookup(pair_rows // nocc_count, occ_energy)
    second_occ = lookup(pair_rows % nocc_count, occ_energy)
    first_vir = lookup(pair_first, vir_energy)
    second_vir = lookup(pair_second, vir_energy)
    denominator = (
        first_occ[None, :] + second_occ[None, :] - first_vir[:, None] - second_vir[:, None]
    )
    return (ladder / denominator).astype(jnp.bfloat16).T


def solution(mesh):
    placed = (P("row", "col"), P("col", "row"), P("col"), P("col"), P(), P())
    return jax.shard_map(
        on_device, mesh=mesh, in_specs=placed, out_specs=P("row", "col"), check_vma=False
    )
```

time: 358 us -> 141 us (0.39)
  waiting for transfers between devices: 321 us -> 64.6 us
  Pallas kernels: 0 us -> 40 us
  starting transfers between devices: 0.04 us -> 26.6 us
  matrix products: 17.5 us -> 0 us
  between operations: 13.5 us -> 0.16 us
  local copies, waits for them, and re-layouts: 0.02 us -> 7.8 us
    reduce_scatter x1 -> x0, waiting for transfers between devices: 200 us -> none  [on_device(): lax.psum_scatter(partial_value, 'col', scatter_dimension=1, tiled=True)]
    all_gather x1 -> x0, waiting for transfers between devices: 120 us -> none  [on_device(): lax.all_gather(integrals, 'row', axis=1, tiled=True)]
    pallas_call x0 -> x5, Pallas kernels: none -> 40 us  [the longest x3 21.9 us: multiply(): pl.pallas_call(kernel, grid=(depth // DEPTH,), in_specs=[pl.BlockSpec((n,...]
    all_to_all x0 -> x1, waiting for transfers between devices: none -> 36.8 us  [on_device(): lax.all_to_all(sums, 'col', split_axis=0, concat_axis=0, tiled=True, axis...]
    ppermute x0 -> x10, waiting for transfers between devices: none -> 27.8 us  [the longest x7 25.5 us: partials(): done[name] = lax.ppermute(block, 'row', row_perm((first[i], second[i])))]
    ppermute x0 -> x10, starting transfers between devices: none -> 18.4 us  [the longest x1 7.9 us: on_device(): a = lax.ppermute(jnp.where(same, own, theirs), ('row', 'col'), swap_perm(0))]
    dot_general x1 -> x0, matrix products: 17.5 us -> none  [on_device(): jnp.dot(amplitudes, lax.all_gather(integrals, 'row', axis=1, tiled=True),...]
    all_to_all x0 -> x1, starting transfers between devices: none -> 8.25 us  [on_device(): lax.all_to_all(sums, 'col', split_axis=0, concat_axis=0, tiled=True, axis...]
  transfers between devices with their start and end apart: 2 -> 11, of which waited for: 2 -> 6; matrix products, arithmetic and copies ran while one was open for 0% -> 0% of each run, Pallas kernels for 0% -> 24%
where the time goes in v1:
time: 141 us; the launch traced here: 140 us
  waiting for transfers between devices  64.6 us (46%)
  Pallas kernels  40 us (28%)
  starting transfers between devices  26.6 us (19%)
  local copies, waits for them, and re-layouts  7.8 us (6%)
    all_to_all x1, waiting for transfers between devices, on_device(): lax.all_to_all(sums, 'col', split_axis=0, concat_axis=0, tiled=True, axis...  36.8 us
    ppermute x7, waiting for transfers between devices, partials(): done[name] = lax.ppermute(block, 'row', row_perm((first[i], second[i])))  25.5 us
    pallas_call x3, Pallas kernels, multiply(): pl.pallas_call(kernel, grid=(depth // DEPTH,), in_specs=[pl.BlockSpec((n,...  21.9 us
    pallas_call x2, Pallas kernels, turned(): pl.pallas_call(turn_kernel, grid=(depth // DEPTH,), in_specs=[pl.BlockSpe...  18.2 us
    all_to_all x1, starting transfers between devices, on_device(): lax.all_to_all(sums, 'col', split_axis=0, concat_axis=0, tiled=True, axis...  8.25 us
    ppermute x1, starting transfers between devices, on_device(): a = lax.ppermute(jnp.where(same, own, theirs), ('row', 'col'), swap_perm(0))  7.9 us
    unnamed x14, local copies, waits for them, and re-layouts  7.8 us
    ppermute x7, starting transfers between devices, partials(): done[name] = lax.ppermute(block, 'row', row_perm((first[i], second[i])))  7.16 us
  transfers between devices with their start and end apart: 11, of which 6 were waited for; matrix products, arithmetic and copies ran while one was open for 0% of the time, Pallas kernels for 24%

profile of v1, /device:TPU:1, one launch (start us, length us, event | category | flops | bytes accessed | tf_op | source)
XLA Modules:
  0.0 140.5 jit_solution(2262649793399020311)
XLA Ops:
  0.0 3.2 %collective-permute-start.4 = (bf16[384,10240]{1,0:T(8,128)(2,1)}, bf16[384,10240]{1,0:T(8,128)(2,1)}, u32[]{:S(2)}, u32[]{:S(2)}) collective-permute-start(bf16[384,10240]{1,0:T(8,128)(2,1)} %rows.1), channel_id=1, source_target_pairs={{0,16},{16,0},{32,48},{48,32},{64,80},{80,64},{96,112},{112,96},{1... | collective-permute-start | bytes 23592968 | tf_op jit(solution)/shard_map/ppermute | solution.py:151
  3.2 0.0 collective-permute-start
  3.2 0.8 collective-permute-start.2
  4.0 1.9 %collective-permute-start.3 = (bf16[64,10240]{1,0:T(8,128)(2,1)}, bf16[64,10240]{1,0:T(8,128)(2,1)}, u32[]{:S(2)}, u32[]{:S(2)}) collective-permute-start(bf16[64,10240]{1,0:T(8,128)(2,1)} %bitcast.5), channel_id=1, source_target_pairs={{0,128},{16,112},{32,160},{48,16},{64,192},{80,48},{96,224},{112,8... | collective-permute-start | bytes 3932168 | tf_op jit(solution)/shard_map/ppermute | solution.py:162
  5.9 9.0 %shard_map.64.refs_4_.refs_3_.refs_1_ = bf16[10240,384]{1,0:T(8,128)(2,1)} custom-call(bf16[384,10240]{1,0:T(8,128)(2,1)} %rows.1), custom_call_target="tpu_custom_call" | custom-call | tf_op jit(solution)/shard_map/pallas_call | solution.py:62
  15.0 16.8 %collective-permute-done.refs_1_ = bf16[64,10240]{1,0:T(8,128)(2,1)} collective-permute-done((bf16[64,10240]{1,0:T(8,128)(2,1)}, bf16[64,10240]{1,0:T(8,128)(2,1)}, u32[]{:S(2)}, u32[]{:S(2)}) %collective-permute-start) | collective-permute-done | bytes 1310752 | tf_op jit(solution)/shard_map/ppermute | solution.py:162
  31.8 0.0 collective-permute-start.1
  31.8 2.7 %collective-permute-start.6 = (bf16[64,10240]{1,0:T(8,128)(2,1)}, bf16[64,10240]{1,0:T(8,128)(2,1)S(1)}, u32[]{:S(2)}, u32[]{:S(2)}) collective-permute-start(bf16[64,10240]{1,0:T(8,128)(2,1)} %collective-permute-done.refs_1_), channel_id=1, source_target_pairs={{0,96},{16,112},{32,0},{48,16},{64,32},{80,48},{96,64},{112,80},{1... | collective-permute-start | bytes 3932168 | tf_op jit(solution)/shard_map/ppermute | solution.py:162
  34.5 0.0 collective-permute-done.2.refs_2_
  34.5 0.0 collective-permute-start.7
  34.5 0.0 collective-permute-done.4.rows
  34.5 9.1 %shard_map.65.refs_5_.refs_4_.refs_2_ = bf16[10240,384]{1,0:T(8,128)(2,1)} custom-call(bf16[384,10240]{1,0:T(8,128)(2,1)} %collective-permute-done.4.rows), custom_call_target="tpu_custom_call" | custom-call | tf_op jit(solution)/shard_map/pallas_call | solution.py:62
  43.6 0.0 collective-permute-done.3.refs_3_
  43.6 0.0 copy-start
  43.6 3.2 %copy-done = bf16[10240,384]{1,0:T(8,128)(2,1)S(1)} copy-done((bf16[10240,384]{1,0:T(8,128)(2,1)S(1)}, bf16[10240,384]{1,0:T(8,128)(2,1)}, u32[]{:S(2)}) %copy-start) | copy-done | bytes 7864344
  46.8 0.0 copy-start.1
  46.8 3.2 %copy-done.1 = bf16[10240,384]{1,0:T(8,128)(2,1)S(1)} copy-done((bf16[10240,384]{1,0:T(8,128)(2,1)S(1)}, bf16[10240,384]{1,0:T(8,128)(2,1)}, u32[]{:S(2)}) %copy-start.1) | copy-done | bytes 7864344
  50.1 0.0 copy-start.2
  50.1 1.3 copy-done.2
  51.4 8.8 %shard_map.66.refs_3_ = f32[256,768]{1,0:T(8,128)S(1)} custom-call(bf16[64,10240]{1,0:T(8,128)(2,1)S(1)} %bitcast.6, bf16[64,10240]{1,0:T(8,128)(2,1)} %collective-permute-done.refs_1_, bf16[64,10240]{1,0:T(8,128)(2,1)} %collective-permute-done.2.refs_2_, bf16[64,10240]{1,0:T(8,128)(2,1)} %collective-permute-done.3.refs_3_, bf16[10240,384]{1,0:T(8,128)(2,1)S(1)} %copy-done, ...), custom_call_target="tpu_custom_call" | custom-call | tf_op jit(solution)/shard_map/pallas_call | solution.py:119
  60.2 0.0 collective-permute-done.1.refs_0_
  60.2 1.8 %collective-permute-start.5 = (bf16[64,10240]{1,0:T(8,128)(2,1)S(1)}, bf16[64,10240]{1,0:T(8,128)(2,1)S(1)}, u32[]{:S(2)}, u32[]{:S(2)}) collective-permute-start(bf16[64,10240]{1,0:T(8,128)(2,1)S(1)} %collective-permute-done.1.refs_0_), channel_id=1, source_target_pairs={{0,96},{16,48},{32,0},{48,80},{64,32},{80,112},{96,64},{112,16},{1... | collective-permute-start | bytes 3932168 | tf_op jit(solution)/shard_map/ppermute | solution.py:162
  62.0 0.0 collective-permute-done.6.refs_1_
  62.0 1.8 %collective-permute-done.7.refs_2_ = bf16[64,10240]{1,0:T(8,128)(2,1)} collective-permute-done((bf16[64,10240]{1,0:T(8,128)(2,1)}, bf16[64,10240]{1,0:T(8,128)(2,1)}, u32[]{:S(2)}, u32[]{:S(2)}) %collective-permute-start.7) | collective-permute-done | bytes 1310752 | tf_op jit(solution)/shard_map/ppermute | solution.py:162
  63.8 7.2 %shard_map.67.refs_4_ = f32[192,768]{1,0:T(8,128)S(1)} custom-call(bf16[64,10240]{1,0:T(8,128)(2,1)S(1)} %collective-permute-done.1.refs_0_, bf16[64,10240]{1,0:T(8,128)(2,1)S(1)} %collective-permute-done.6.refs_1_, bf16[64,10240]{1,0:T(8,128)(2,1)} %collective-permute-done.7.refs_2_, bf16[10240,384]{1,0:T(8,128)(2,1)S(1)} %copy-done, ...), custom_call_target="tpu_custom_call" | custom-call | tf_op jit(solution)/shard_map/pallas_call | solution.py:119
  71.1 6.9 %collective-permute-done.5.refs_0_ = bf16[64,10240]{1,0:T(8,128)(2,1)S(1)} collective-permute-done((bf16[64,10240]{1,0:T(8,128)(2,1)S(1)}, bf16[64,10240]{1,0:T(8,128)(2,1)S(1)}, u32[]{:S(2)}, u32[]{:S(2)}) %collective-permute-start.5) | collective-permute-done | bytes 1310752 | tf_op jit(solution)/shard_map/ppermute | solution.py:162
  77.9 5.9 %shard_map.68 = f32[8,64,768]{2,1,0:T(8,128)} custom-call(bf16[64,10240]{1,0:T(8,128)(2,1)S(1)} %collective-permute-done.5.refs_0_, bf16[10240,384]{1,0:T(8,128)(2,1)S(1)} %copy-done, bf16[10240,384]{1,0:T(8,128)(2,1)S(1)} %copy-done.1, f32[256,768]{1,0:T(8,128)S(1)} %shard_map.66.refs_3_, f32[192,768]{1,0:T(8,128)S(1)} %shard_map.67.refs_4_), custom_call_target="tpu_custom_call" | custom-call | tf_op jit(solution)/shard_map/pallas_call | solution.py:119
  83.8 0.0 copy-start.4
  83.8 8.3 %all-to-all-start = ((f32[8,64,768]{2,1,0:T(8,128)}), f32[8,64,768]{2,1,0:T(8,128)S(1)}, u32[]{:S(2)}, u32[]{:S(2)}) async-start(f32[8,64,768]{2,1,0:T(8,128)} %shard_map.68), calls=%async_computation | async-start | bytes 3145728 | tf_op jit(solution)/shard_map/all_to_all | solution.py:187
  92.1 0.0 copy-start.3
  92.1 0.0 copy-start.5
  92.1 0.0 copy-start.6
  92.1 0.0 copy-done.4
  92.1 0.2 select_reduce_fusion.2
  92.3 36.8 %all-to-all-done = f32[8,64,768]{2,1,0:T(8,128)S(1)} async-done(((f32[8,64,768]{2,1,0:T(8,128)}), f32[8,64,768]{2,1,0:T(8,128)S(1)}, u32[]{:S(2)}, u32[]{:S(2)}) %all-to-all-start) | async-done | bytes 1572896 | tf_op jit(solution)/shard_map/all_to_all | solution.py:187
  129.2 0.1 reduce_sum.45
  129.3 7.9 %collective-permute-start.8 = (f32[64,384]{1,0:T(8,128)S(1)}, f32[64,384]{1,0:T(8,128)S(1)}, u32[]{:S(2)}, u32[]{:S(2)}) collective-permute-start(f32[64,384]{1,0:T(8,128)S(1)} %get-tuple-element.20), channel_id=1, source_target_pairs={{0,0},{1,16},{2,2},{3,18},{4,4},{5,20},{6,6},{7,22},{8,8},{9,24},{... | collective-permute-start | bytes 294920 | tf_op jit(solution)/shard_map/ppermute | solution.py:190
  137.2 0.1 collective-permute-start.9
  137.3 0.0 copy-done.3
  137.3 0.0 copy-done.5
  137.3 0.0 copy-done.6
  137.3 0.3 select_reduce_fusion.1
  137.6 1.9 %collective-permute-done.8 = f32[64,384]{1,0:T(8,128)S(1)} collective-permute-done((f32[64,384]{1,0:T(8,128)S(1)}, f32[64,384]{1,0:T(8,128)S(1)}, u32[]{:S(2)}, u32[]{:S(2)}) %collective-permute-start.8) | collective-permute-done | bytes 98336 | tf_op jit(solution)/shard_map/ppermute | solution.py:190
  139.5 0.3 collective-permute-done.9
  139.8 0.7 fusion
  (3 shorter events, 0.0 us)
Async XLA Ops:
  0.0 34.5 %collective-permute-start.4 = (bf16[384,10240]{1,0:T(8,128)(2,1)}, bf16[384,10240]{1,0:T(8,128)(2,1)}, u32[]{:S(2)}, u32[]{:S(2)}) collective-permute-start(bf16[384,10240]{1,0:T(8,128)(2,1)} %rows.1), channel_id=1, source_target_pairs={{0,16},{16,0},{32,48},{48,32},{64,80},{80,64},{96,112},{112,96},{1... | collective-permute-start | bytes 23592968 | tf_op jit(solution)/shard_map/ppermute | solution.py:151
  3.2 28.6 %collective-permute-start = (bf16[64,10240]{1,0:T(8,128)(2,1)}, bf16[64,10240]{1,0:T(8,128)(2,1)}, u32[]{:S(2)}, u32[]{:S(2)}) collective-permute-start(bf16[64,10240]{1,0:T(8,128)(2,1)} %bitcast.3), channel_id=1, source_target_pairs={{0,96},{16,144},{32,0},{48,176},{64,32},{80,208},{96,64},{112,240}... | collective-permute-start | bytes 3932168 | tf_op jit(solution)/shard_map/ppermute | solution.py:162
  3.2 31.2 %collective-permute-start.2 = (bf16[64,10240]{1,0:T(8,128)(2,1)}, bf16[64,10240]{1,0:T(8,128)(2,1)}, u32[]{:S(2)}, u32[]{:S(2)}) collective-permute-start(bf16[64,10240]{1,0:T(8,128)(2,1)} %bitcast.4), channel_id=1, source_target_pairs={{0,32},{16,48},{32,64},{48,80},{64,96},{80,112},{96,0},{112,16},{1... | collective-permute-start | bytes 3932168 | tf_op jit(solution)/shard_map/ppermute | solution.py:162
  4.0 39.6 %collective-permute-start.3 = (bf16[64,10240]{1,0:T(8,128)(2,1)}, bf16[64,10240]{1,0:T(8,128)(2,1)}, u32[]{:S(2)}, u32[]{:S(2)}) collective-permute-start(bf16[64,10240]{1,0:T(8,128)(2,1)} %bitcast.5), channel_id=1, source_target_pairs={{0,128},{16,112},{32,160},{48,16},{64,192},{80,48},{96,224},{112,8... | collective-permute-start | bytes 3932168 | tf_op jit(solution)/shard_map/ppermute | solution.py:162
  31.8 28.4 %collective-permute-start.1 = (bf16[64,10240]{1,0:T(8,128)(2,1)}, bf16[64,10240]{1,0:T(8,128)(2,1)S(1)}, u32[]{:S(2)}, u32[]{:S(2)}) collective-permute-start(bf16[64,10240]{1,0:T(8,128)(2,1)} %collective-permute-done.refs_1_), channel_id=1, source_target_pairs={{0,128},{16,48},{32,160},{48,80},{64,192},{80,112},{96,224},{112,1... | collective-permute-start | bytes 3932168 | tf_op jit(solution)/shard_map/ppermute | solution.py:162
  31.8 30.2 %collective-permute-start.6 = (bf16[64,10240]{1,0:T(8,128)(2,1)}, bf16[64,10240]{1,0:T(8,128)(2,1)S(1)}, u32[]{:S(2)}, u32[]{:S(2)}) collective-permute-start(bf16[64,10240]{1,0:T(8,128)(2,1)} %collective-permute-done.refs_1_), channel_id=1, source_target_pairs={{0,96},{16,112},{32,0},{48,16},{64,32},{80,48},{96,64},{112,80},{1... | collective-permute-start | bytes 3932168 | tf_op jit(solution)/shard_map/ppermute | solution.py:162
  34.5 29.3 %collective-permute-start.7 = (bf16[64,10240]{1,0:T(8,128)(2,1)}, bf16[64,10240]{1,0:T(8,128)(2,1)}, u32[]{:S(2)}, u32[]{:S(2)}) collective-permute-start(bf16[64,10240]{1,0:T(8,128)(2,1)} %collective-permute-done.2.refs_2_), channel_id=1, source_target_pairs={{0,128},{16,48},{32,160},{48,80},{64,192},{80,112},{96,224},{112,1... | collective-permute-start | bytes 3932168 | tf_op jit(solution)/shard_map/ppermute | solution.py:162
  43.6 3.2 %copy-start = (bf16[10240,384]{1,0:T(8,128)(2,1)S(1)}, bf16[10240,384]{1,0:T(8,128)(2,1)}, u32[]{:S(2)}) copy-start(bf16[10240,384]{1,0:T(8,128)(2,1)} %shard_map.64.refs_4_.refs_3_.refs_1_) | copy-start | bytes 23592964
  46.8 3.2 %copy-start.1 = (bf16[10240,384]{1,0:T(8,128)(2,1)S(1)}, bf16[10240,384]{1,0:T(8,128)(2,1)}, u32[]{:S(2)}) copy-start(bf16[10240,384]{1,0:T(8,128)(2,1)} %shard_map.65.refs_5_.refs_4_.refs_2_) | copy-start | bytes 23592964
  50.1 1.3 copy-start.2
  60.2 17.7 %collective-permute-start.5 = (bf16[64,10240]{1,0:T(8,128)(2,1)S(1)}, bf16[64,10240]{1,0:T(8,128)(2,1)S(1)}, u32[]{:S(2)}, u32[]{:S(2)}) collective-permute-start(bf16[64,10240]{1,0:T(8,128)(2,1)S(1)} %collective-permute-done.1.refs_0_), channel_id=1, source_target_pairs={{0,96},{16,48},{32,0},{48,80},{64,32},{80,112},{96,64},{112,16},{1... | collective-permute-start | bytes 3932168 | tf_op jit(solution)/shard_map/ppermute | solution.py:162
  83.8 8.3 %copy-start.4 = (f32[200]{0:T(256)S(1)}, f32[200]{0:T(256)}, u32[]{:S(2)}) copy-start(f32[200]{0:T(256)} %param.10) | copy-start | bytes 2404
  83.8 45.3 %all-to-all-start = ((f32[8,64,768]{2,1,0:T(8,128)}), f32[8,64,768]{2,1,0:T(8,128)S(1)}, u32[]{:S(2)}, u32[]{:S(2)}) async-start(f32[8,64,768]{2,1,0:T(8,128)} %shard_map.68), calls=%async_computation | async-start | bytes 3145728 | tf_op jit(solution)/shard_map/all_to_all | solution.py:187
  92.1 45.2 %copy-start.3 = (f32[1600]{0:T(1024)S(1)}, f32[1600]{0:T(1024)}, u32[]{:S(2)}) copy-start(f32[1600]{0:T(1024)} %param.11) | copy-start | bytes 19204
  92.1 45.2 %copy-start.5 = (s32[64]{0:T(128)S(1)}, s32[64]{0:T(128)}, u32[]{:S(2)}) copy-start(s32[64]{0:T(128)} %param.8) | copy-start | bytes 772
  92.1 45.2 %copy-start.6 = (s32[64]{0:T(128)S(1)}, s32[64]{0:T(128)}, u32[]{:S(2)}) copy-start(s32[64]{0:T(128)} %param.9) | copy-start | bytes 772
  129.3 10.2 %collective-permute-start.8 = (f32[64,384]{1,0:T(8,128)S(1)}, f32[64,384]{1,0:T(8,128)S(1)}, u32[]{:S(2)}, u32[]{:S(2)}) collective-permute-start(f32[64,384]{1,0:T(8,128)S(1)} %get-tuple-element.20), channel_id=1, source_target_pairs={{0,0},{1,16},{2,2},{3,18},{4,4},{5,20},{6,6},{7,22},{8,8},{9,24},{... | collective-permute-start | bytes 294920 | tf_op jit(solution)/shard_map/ppermute | solution.py:190
  137.2 2.6 %collective-permute-start.9 = (f32[64,384]{1,0:T(8,128)S(1)}, f32[64,384]{1,0:T(8,128)S(1)}, u32[]{:S(2)}, u32[]{:S(2)}) collective-permute-start(f32[64,384]{1,0:T(8,128)S(1)} %get-tuple-element.19), channel_id=1, source_target_pairs={{0,16},{1,0},{2,18},{3,2},{4,20},{5,4},{6,22},{7,6},{8,24},{9,8},{... | collective-permute-start | bytes 294920 | tf_op jit(solution)/shard_map/ppermute | solution.py:191

commit v2 on v1

--- a/solution.py
+++ b/solution.py
@@ -10,6 +10,8 @@
 YS, ZS = 4, 8
 STEP = {"x": (1, 0), "U": (0, 1), "D": (0, -1)}
 SLICES = ((64, (0, 0, 0, 1, 1, 2, 4), "DUxxDxD", "xUDUDUU"),)
+UNITS = 32767.0
+SMALLEST = 2.0**-126
 DEPTH = 2048
 GROUPS = (((0, 4), (4, 7), (7, 8)),)
 ORDER = (
@@ -89,6 +91,25 @@
 def product_kernel(*refs):
     *blocks, own, other, total = refs
     accumulate(total, blocks, (own, other))
+
+
+def coded(sums):
+    largest = jnp.maximum(jnp.max(jnp.abs(sums), axis=1, keepdims=True), SMALLEST)
+    power = jnp.clip(jnp.floor(jnp.log2(largest)) + 1.0, -126.0, 126.0)
+    scaled = sums * jnp.exp2(-power)
+    part = jnp.ceil(largest * jnp.exp2(-power) * 256.0)
+    whole = jnp.round(scaled * (256.0 * UNITS / part))
+    place = lax.broadcasted_iota(jnp.int32, (sums.shape[0], 128), 1)
+    note = jnp.where(place == 0, power, part)
+    return jnp.concatenate([whole, note], axis=1).astype(jnp.int32).astype(jnp.int16)
+
+
+def decoded(shares):
+    width = shares.shape[-1] - 128
+    whole = shares[..., :width].astype(jnp.float32)
+    power = shares[..., width : width + 1].astype(jnp.float32)
+    part = shares[..., width + 1 : width + 2].astype(jnp.float32)
+    return whole * (part * (1.0 / (256.0 * UNITS))) * jnp.exp2(power)
 
 
 def finish_kernel(counts, spots, *refs):
@@ -108,11 +129,11 @@
                 (x0, y0), (x1, y1) = spots[0][i], spots[1][i]
                 from_x = jnp.where(core == 0, x ^ x0, x ^ x1)
                 from_y = jnp.where(core == 0, (y + YS - y0) % YS, (y + YS - y1) % YS)
-                out[from_x * YS + from_y] = sums[j * n : (j + 1) * n, :]
+                out[from_x * YS + from_y] = coded(sums[j * n : (j + 1) * n, :])
                 i += 1
 
 
-def multiply(kernel, blocks, own, other, earlier, out_shape, scratch):
+def multiply(kernel, blocks, own, other, earlier, out_shape, scratch, kind=jnp.float32):
     n, depth = blocks[0].shape
     rows = own.shape[1]
     whole = lambda shape: pl.BlockSpec(shape, lambda k: (0,) * len(shape))
@@ -123,7 +144,7 @@
         + [pl.BlockSpec((DEPTH, rows), lambda k: (k, 0))] * 2
         + [whole(sums.shape) for sums in earlier],
         out_specs=whole(out_shape),
-        out_shape=jax.ShapeDtypeStruct(out_shape, jnp.float32),
+        out_shape=jax.ShapeDtypeStruct(out_shape, kind),
         scratch_shapes=scratch,
         compiler_params=pltpu.CompilerParams(vmem_limit_bytes=16 * 1024 * 1024),
         cost_estimate=pl.CostEstimate(flops=0, bytes_accessed=0, transcendentals=0),
@@ -140,7 +161,7 @@
     counts = tuple(b - a for a, b in groups)
     kernel = functools.partial(finish_kernel, counts, spots)
     scratch = [pltpu.VMEM((len(blocks) * n, width), jnp.float32)]
-    return multiply(kernel, blocks, own, other, earlier, (8, n, width), scratch)
+    return multiply(kernel, blocks, own, other, earlier, (8, n, width + 128), scratch, jnp.int16)
 
 
 def after(value, *others):
@@ -185,7 +206,7 @@
         if done:
             sums = after(sums, shares)
         shares = lax.all_to_all(sums, "col", split_axis=0, concat_axis=0, tiled=True, axis_index_groups=along_z)
-        mine = jnp.sum(shares, axis=0)
+        mine = jnp.sum(decoded(shares), axis=0)
         own, theirs = mine[:, :local_rows], mine[:, local_rows:]
         a = lax.ppermute(jnp.where(same, own, theirs), ("row", "col"), swap_perm(0))
         b = lax.ppermute(jnp.where(same, theirs, own), ("row", "col"), swap_perm(1))

time: 141 us -> 128 us (0.908)
  waiting for transfers between devices: 64.6 us -> 50.1 us
    all_to_all x1, waiting for transfers between devices: 36.8 us -> 22.4 us  [on_device(): lax.all_to_all(sums, 'col', split_axis=0, concat_axis=0, tiled=True, axis...]
  transfers between devices with their start and end apart: 11 -> 11, of which waited for: 6 -> 6; matrix products, arithmetic and copies ran while one was open for 0% -> 0% of each run, Pallas kernels for 24% -> 27%
where the time goes in v2:
time: 128 us; the launch traced here: 127 us
  waiting for transfers between devices  50.1 us (39%)
  Pallas kernels  40.1 us (31%)
  starting transfers between devices  27.1 us (21%)
  local copies, waits for them, and re-layouts  7.8 us (6%)
  other arithmetic  1.86 us (1%)
    ppermute x7, waiting for transfers between devices, partials(): done[name] = lax.ppermute(block, 'row', row_perm((first[i], second[i])))  25.5 us
    all_to_all x1, waiting for transfers between devices, on_device(): lax.all_to_all(sums, 'col', split_axis=0, concat_axis=0, tiled=True, axis...  22.4 us
    pallas_call x3, Pallas kernels, multiply(): pl.pallas_call(kernel, grid=(depth // DEPTH,), in_specs=[pl.BlockSpec((n,...  21.9 us
    pallas_call x2, Pallas kernels, turned(): pl.pallas_call(turn_kernel, grid=(depth // DEPTH,), in_specs=[pl.BlockSpe...  18.2 us
    ppermute x1, starting transfers between devices, on_device(): a = lax.ppermute(jnp.where(same, own, theirs), ('row', 'col'), swap_perm(0))  8.38 us
    all_to_all x1, starting transfers between devices, on_device(): lax.all_to_all(sums, 'col', split_axis=0, concat_axis=0, tiled=True, axis...  8.28 us
    unnamed x14, local copies, waits for them, and re-layouts  7.8 us
    ppermute x7, starting transfers between devices, partials(): done[name] = lax.ppermute(block, 'row', row_perm((first[i], second[i])))  7.16 us
  transfers between devices with their start and end apart: 11, of which 6 were waited for; matrix products, arithmetic and copies ran while one was open for 0% of the time, Pallas kernels for 27%

profile of v2, /device:TPU:1, one launch (start us, length us, event | category | flops | bytes accessed | tf_op | source)
XLA Modules:
  0.0 127.1 jit_solution(15523562911250906977)
XLA Ops:
  0.0 3.2 %collective-permute-start.4 = (bf16[384,10240]{1,0:T(8,128)(2,1)}, bf16[384,10240]{1,0:T(8,128)(2,1)}, u32[]{:S(2)}, u32[]{:S(2)}) collective-permute-start(bf16[384,10240]{1,0:T(8,128)(2,1)} %rows.1), channel_id=1, source_target_pairs={{0,16},{16,0},{32,48},{48,32},{64,80},{80,64},{96,112},{112,96},{1... | collective-permute-start | bytes 23592968 | tf_op jit(solution)/shard_map/ppermute | solution.py:172
  3.2 0.0 collective-permute-start
  3.2 0.8 collective-permute-start.2
  4.0 1.9 %collective-permute-start.3 = (bf16[64,10240]{1,0:T(8,128)(2,1)}, bf16[64,10240]{1,0:T(8,128)(2,1)}, u32[]{:S(2)}, u32[]{:S(2)}) collective-permute-start(bf16[64,10240]{1,0:T(8,128)(2,1)} %bitcast.5), channel_id=1, source_target_pairs={{0,128},{16,112},{32,160},{48,16},{64,192},{80,48},{96,224},{112,8... | collective-permute-start | bytes 3932168 | tf_op jit(solution)/shard_map/ppermute | solution.py:183
  5.9 9.1 %shard_map.64.refs_4_.refs_3_.refs_1_ = bf16[10240,384]{1,0:T(8,128)(2,1)} custom-call(bf16[384,10240]{1,0:T(8,128)(2,1)} %rows.1), custom_call_target="tpu_custom_call" | custom-call | tf_op jit(solution)/shard_map/pallas_call | solution.py:64
  15.0 16.8 %collective-permute-done.refs_1_ = bf16[64,10240]{1,0:T(8,128)(2,1)} collective-permute-done((bf16[64,10240]{1,0:T(8,128)(2,1)}, bf16[64,10240]{1,0:T(8,128)(2,1)}, u32[]{:S(2)}, u32[]{:S(2)}) %collective-permute-start) | collective-permute-done | bytes 1310752 | tf_op jit(solution)/shard_map/ppermute | solution.py:183
  31.8 0.0 collective-permute-start.1
  31.8 2.7 %collective-permute-start.6 = (bf16[64,10240]{1,0:T(8,128)(2,1)}, bf16[64,10240]{1,0:T(8,128)(2,1)S(1)}, u32[]{:S(2)}, u32[]{:S(2)}) collective-permute-start(bf16[64,10240]{1,0:T(8,128)(2,1)} %collective-permute-done.refs_1_), channel_id=1, source_target_pairs={{0,96},{16,112},{32,0},{48,16},{64,32},{80,48},{96,64},{112,80},{1... | collective-permute-start | bytes 3932168 | tf_op jit(solution)/shard_map/ppermute | solution.py:183
  34.5 0.0 collective-permute-done.2.refs_2_
  34.5 0.0 collective-permute-start.7
  34.5 0.0 collective-permute-done.4.rows
  34.5 9.1 %shard_map.65.refs_5_.refs_4_.refs_2_ = bf16[10240,384]{1,0:T(8,128)(2,1)} custom-call(bf16[384,10240]{1,0:T(8,128)(2,1)} %collective-permute-done.4.rows), custom_call_target="tpu_custom_call" | custom-call | tf_op jit(solution)/shard_map/pallas_call | solution.py:64
  43.6 0.0 collective-permute-done.3.refs_3_
  43.6 0.0 copy-start
  43.6 3.2 %copy-done = bf16[10240,384]{1,0:T(8,128)(2,1)S(1)} copy-done((bf16[10240,384]{1,0:T(8,128)(2,1)S(1)}, bf16[10240,384]{1,0:T(8,128)(2,1)}, u32[]{:S(2)}) %copy-start) | copy-done | bytes 7864344
  46.8 0.0 copy-start.1
  46.8 3.2 %copy-done.1 = bf16[10240,384]{1,0:T(8,128)(2,1)S(1)} copy-done((bf16[10240,384]{1,0:T(8,128)(2,1)S(1)}, bf16[10240,384]{1,0:T(8,128)(2,1)}, u32[]{:S(2)}) %copy-start.1) | copy-done | bytes 7864344
  50.1 0.0 copy-start.2
  50.1 1.3 %copy-done.2 = bf16[10240,64]{0,1:T(8,128)(2,1)S(1)} copy-done((bf16[10240,64]{0,1:T(8,128)(2,1)S(1)}, bf16[10240,64]{0,1:T(8,128)(2,1)}, u32[]{:S(2)}) %copy-start.2) | copy-done | bytes 1310744
  51.4 8.8 %shard_map.66.refs_3_ = f32[256,768]{1,0:T(8,128)S(1)} custom-call(bf16[64,10240]{1,0:T(8,128)(2,1)S(1)} %bitcast.6, bf16[64,10240]{1,0:T(8,128)(2,1)} %collective-permute-done.refs_1_, bf16[64,10240]{1,0:T(8,128)(2,1)} %collective-permute-done.2.refs_2_, bf16[64,10240]{1,0:T(8,128)(2,1)} %collective-permute-done.3.refs_3_, bf16[10240,384]{1,0:T(8,128)(2,1)S(1)} %copy-done, ...), custom_call_target="tpu_custom_call" | custom-call | tf_op jit(solution)/shard_map/pallas_call | solution.py:140
  60.2 0.0 collective-permute-done.1.refs_0_
  60.2 1.8 %collective-permute-start.5 = (bf16[64,10240]{1,0:T(8,128)(2,1)S(1)}, bf16[64,10240]{1,0:T(8,128)(2,1)S(1)}, u32[]{:S(2)}, u32[]{:S(2)}) collective-permute-start(bf16[64,10240]{1,0:T(8,128)(2,1)S(1)} %collective-permute-done.1.refs_0_), channel_id=1, source_target_pairs={{0,96},{16,48},{32,0},{48,80},{64,32},{80,112},{96,64},{112,16},{1... | collective-permute-start | bytes 3932168 | tf_op jit(solution)/shard_map/ppermute | solution.py:183
  62.0 0.0 collective-permute-done.6.refs_1_
  62.0 1.8 %collective-permute-done.7.refs_2_ = bf16[64,10240]{1,0:T(8,128)(2,1)} collective-permute-done((bf16[64,10240]{1,0:T(8,128)(2,1)}, bf16[64,10240]{1,0:T(8,128)(2,1)}, u32[]{:S(2)}, u32[]{:S(2)}) %collective-permute-start.7) | collective-permute-done | bytes 1310752 | tf_op jit(solution)/shard_map/ppermute | solution.py:183
  63.8 7.2 %shard_map.67.refs_4_ = f32[192,768]{1,0:T(8,128)S(1)} custom-call(bf16[64,10240]{1,0:T(8,128)(2,1)S(1)} %collective-permute-done.1.refs_0_, bf16[64,10240]{1,0:T(8,128)(2,1)S(1)} %collective-permute-done.6.refs_1_, bf16[64,10240]{1,0:T(8,128)(2,1)} %collective-permute-done.7.refs_2_, bf16[10240,384]{1,0:T(8,128)(2,1)S(1)} %copy-done, ...), custom_call_target="tpu_custom_call" | custom-call | tf_op jit(solution)/shard_map/pallas_call | solution.py:140
  71.1 6.9 %collective-permute-done.5.refs_0_ = bf16[64,10240]{1,0:T(8,128)(2,1)S(1)} collective-permute-done((bf16[64,10240]{1,0:T(8,128)(2,1)S(1)}, bf16[64,10240]{1,0:T(8,128)(2,1)S(1)}, u32[]{:S(2)}, u32[]{:S(2)}) %collective-permute-start.5) | collective-permute-done | bytes 1310752 | tf_op jit(solution)/shard_map/ppermute | solution.py:183
  77.9 5.9 %shard_map.68 = s16[8,64,896]{2,1,0:T(8,128)(2,1)} custom-call(bf16[64,10240]{1,0:T(8,128)(2,1)S(1)} %collective-permute-done.5.refs_0_, bf16[10240,384]{1,0:T(8,128)(2,1)S(1)} %copy-done, bf16[10240,384]{1,0:T(8,128)(2,1)S(1)} %copy-done.1, f32[256,768]{1,0:T(8,128)S(1)} %shard_map.66.refs_3_, f32[192,768]{1,0:T(8,128)S(1)} %shard_map.67.refs_4_), custom_call_target="tpu_custom_call" | custom-call | tf_op jit(solution)/shard_map/pallas_call | solution.py:140
  83.9 0.0 copy-start.4
  83.9 0.0 copy-start.3
  83.9 0.0 copy-start.5
  83.9 0.0 copy-start.6
  83.9 8.3 %all-to-all-start = ((s16[8,64,896]{2,1,0:T(8,128)(2,1)}), s16[8,64,896]{2,1,0:T(8,128)(2,1)S(1)}, u32[]{:S(2)}, u32[]{:S(2)}) async-start(s16[8,64,896]{2,1,0:T(8,128)(2,1)} %shard_map.68), calls=%async_computation | async-start | bytes 1835008 | tf_op jit(solution)/shard_map/all_to_all | solution.py:208
  92.2 0.0 copy-done.4
  92.2 0.2 select_reduce_fusion.2
  92.3 22.4 %all-to-all-done = s16[8,64,896]{2,1,0:T(8,128)(2,1)S(1)} async-done(((s16[8,64,896]{2,1,0:T(8,128)(2,1)}), s16[8,64,896]{2,1,0:T(8,128)(2,1)S(1)}, u32[]{:S(2)}, u32[]{:S(2)}) %all-to-all-start) | async-done | bytes 917536 | tf_op jit(solution)/shard_map/all_to_all | solution.py:208
  114.7 0.3 multiply_reduce_fusion.1
  115.1 0.4 multiply_reduce_fusion
  115.4 8.4 %collective-permute-start.8 = (f32[64,384]{1,0:T(8,128)S(1)}, f32[64,384]{1,0:T(8,128)S(1)}, u32[]{:S(2)}, u32[]{:S(2)}) collective-permute-start(f32[64,384]{1,0:T(8,128)S(1)} %get-tuple-element.22), channel_id=1, source_target_pairs={{0,0},{1,16},{2,2},{3,18},{4,4},{5,20},{6,6},{7,22},{8,8},{9,24},{... | collective-permute-start | bytes 294920 | tf_op jit(solution)/shard_map/ppermute | solution.py:211
  123.8 0.1 collective-permute-start.9
  123.9 0.0 copy-done.3
  123.9 0.0 copy-done.5
  124.0 0.0 copy-done.6
  124.0 0.3 select_reduce_fusion.1
  124.2 1.9 %collective-permute-done.8 = f32[64,384]{1,0:T(8,128)S(1)} collective-permute-done((f32[64,384]{1,0:T(8,128)S(1)}, f32[64,384]{1,0:T(8,128)S(1)}, u32[]{:S(2)}, u32[]{:S(2)}) %collective-permute-start.8) | collective-permute-done | bytes 98336 | tf_op jit(solution)/shard_map/ppermute | solution.py:211
  126.1 0.3 collective-permute-done.9
  126.4 0.7 fusion
  (3 shorter events, 0.0 us)
Async XLA Ops:
  0.0 34.5 %collective-permute-start.4 = (bf16[384,10240]{1,0:T(8,128)(2,1)}, bf16[384,10240]{1,0:T(8,128)(2,1)}, u32[]{:S(2)}, u32[]{:S(2)}) collective-permute-start(bf16[384,10240]{1,0:T(8,128)(2,1)} %rows.1), channel_id=1, source_target_pairs={{0,16},{16,0},{32,48},{48,32},{64,80},{80,64},{96,112},{112,96},{1... | collective-permute-start | bytes 23592968 | tf_op jit(solution)/shard_map/ppermute | solution.py:172
  3.2 28.6 %collective-permute-start = (bf16[64,10240]{1,0:T(8,128)(2,1)}, bf16[64,10240]{1,0:T(8,128)(2,1)}, u32[]{:S(2)}, u32[]{:S(2)}) collective-permute-start(bf16[64,10240]{1,0:T(8,128)(2,1)} %bitcast.3), channel_id=1, source_target_pairs={{0,96},{16,144},{32,0},{48,176},{64,32},{80,208},{96,64},{112,240}... | collective-permute-start | bytes 3932168 | tf_op jit(solution)/shard_map/ppermute | solution.py:183
  3.2 31.2 %collective-permute-start.2 = (bf16[64,10240]{1,0:T(8,128)(2,1)}, bf16[64,10240]{1,0:T(8,128)(2,1)}, u32[]{:S(2)}, u32[]{:S(2)}) collective-permute-start(bf16[64,10240]{1,0:T(8,128)(2,1)} %bitcast.4), channel_id=1, source_target_pairs={{0,32},{16,48},{32,64},{48,80},{64,96},{80,112},{96,0},{112,16},{1... | collective-permute-start | bytes 3932168 | tf_op jit(solution)/shard_map/ppermute | solution.py:183
  4.0 39.6 %collective-permute-start.3 = (bf16[64,10240]{1,0:T(8,128)(2,1)}, bf16[64,10240]{1,0:T(8,128)(2,1)}, u32[]{:S(2)}, u32[]{:S(2)}) collective-permute-start(bf16[64,10240]{1,0:T(8,128)(2,1)} %bitcast.5), channel_id=1, source_target_pairs={{0,128},{16,112},{32,160},{48,16},{64,192},{80,48},{96,224},{112,8... | collective-permute-start | bytes 3932168 | tf_op jit(solution)/shard_map/ppermute | solution.py:183
  31.8 28.4 %collective-permute-start.1 = (bf16[64,10240]{1,0:T(8,128)(2,1)}, bf16[64,10240]{1,0:T(8,128)(2,1)S(1)}, u32[]{:S(2)}, u32[]{:S(2)}) collective-permute-start(bf16[64,10240]{1,0:T(8,128)(2,1)} %collective-permute-done.refs_1_), channel_id=1, source_target_pairs={{0,128},{16,48},{32,160},{48,80},{64,192},{80,112},{96,224},{112,1... | collective-permute-start | bytes 3932168 | tf_op jit(solution)/shard_map/ppermute | solution.py:183
  31.8 30.2 %collective-permute-start.6 = (bf16[64,10240]{1,0:T(8,128)(2,1)}, bf16[64,10240]{1,0:T(8,128)(2,1)S(1)}, u32[]{:S(2)}, u32[]{:S(2)}) collective-permute-start(bf16[64,10240]{1,0:T(8,128)(2,1)} %collective-permute-done.refs_1_), channel_id=1, source_target_pairs={{0,96},{16,112},{32,0},{48,16},{64,32},{80,48},{96,64},{112,80},{1... | collective-permute-start | bytes 3932168 | tf_op jit(solution)/shard_map/ppermute | solution.py:183
  34.5 29.3 %collective-permute-start.7 = (bf16[64,10240]{1,0:T(8,128)(2,1)}, bf16[64,10240]{1,0:T(8,128)(2,1)}, u32[]{:S(2)}, u32[]{:S(2)}) collective-permute-start(bf16[64,10240]{1,0:T(8,128)(2,1)} %collective-permute-done.2.refs_2_), channel_id=1, source_target_pairs={{0,128},{16,48},{32,160},{48,80},{64,192},{80,112},{96,224},{112,1... | collective-permute-start | bytes 3932168 | tf_op jit(solution)/shard_map/ppermute | solution.py:183
  43.6 3.2 %copy-start = (bf16[10240,384]{1,0:T(8,128)(2,1)S(1)}, bf16[10240,384]{1,0:T(8,128)(2,1)}, u32[]{:S(2)}) copy-start(bf16[10240,384]{1,0:T(8,128)(2,1)} %shard_map.64.refs_4_.refs_3_.refs_1_) | copy-start | bytes 23592964
  46.8 3.2 %copy-start.1 = (bf16[10240,384]{1,0:T(8,128)(2,1)S(1)}, bf16[10240,384]{1,0:T(8,128)(2,1)}, u32[]{:S(2)}) copy-start(bf16[10240,384]{1,0:T(8,128)(2,1)} %shard_map.65.refs_5_.refs_4_.refs_2_) | copy-start | bytes 23592964
  50.1 1.3 %copy-start.2 = (bf16[10240,64]{0,1:T(8,128)(2,1)S(1)}, bf16[10240,64]{0,1:T(8,128)(2,1)}, u32[]{:S(2)}) copy-start(bf16[10240,64]{0,1:T(8,128)(2,1)} %param.7) | copy-start | bytes 3932164
  60.2 17.7 %collective-permute-start.5 = (bf16[64,10240]{1,0:T(8,128)(2,1)S(1)}, bf16[64,10240]{1,0:T(8,128)(2,1)S(1)}, u32[]{:S(2)}, u32[]{:S(2)}) collective-permute-start(bf16[64,10240]{1,0:T(8,128)(2,1)S(1)} %collective-permute-done.1.refs_0_), channel_id=1, source_target_pairs={{0,96},{16,48},{32,0},{48,80},{64,32},{80,112},{96,64},{112,16},{1... | collective-permute-start | bytes 3932168 | tf_op jit(solution)/shard_map/ppermute | solution.py:183
  83.9 8.3 %copy-start.4 = (f32[200]{0:T(256)S(1)}, f32[200]{0:T(256)}, u32[]{:S(2)}) copy-start(f32[200]{0:T(256)} %param.10) | copy-start | bytes 2404
  83.9 40.1 %copy-start.3 = (f32[1600]{0:T(1024)S(1)}, f32[1600]{0:T(1024)}, u32[]{:S(2)}) copy-start(f32[1600]{0:T(1024)} %param.11) | copy-start | bytes 19204
  83.9 40.1 %copy-start.5 = (s32[64]{0:T(128)S(1)}, s32[64]{0:T(128)}, u32[]{:S(2)}) copy-start(s32[64]{0:T(128)} %param.8) | copy-start | bytes 772
  83.9 40.1 %copy-start.6 = (s32[64]{0:T(128)S(1)}, s32[64]{0:T(128)}, u32[]{:S(2)}) copy-start(s32[64]{0:T(128)} %param.9) | copy-start | bytes 772
  83.9 30.8 %all-to-all-start = ((s16[8,64,896]{2,1,0:T(8,128)(2,1)}), s16[8,64,896]{2,1,0:T(8,128)(2,1)S(1)}, u32[]{:S(2)}, u32[]{:S(2)}) async-start(s16[8,64,896]{2,1,0:T(8,128)(2,1)} %shard_map.68), calls=%async_computation | async-start | bytes 1835008 | tf_op jit(solution)/shard_map/all_to_all | solution.py:208
  115.4 10.7 %collective-permute-start.8 = (f32[64,384]{1,0:T(8,128)S(1)}, f32[64,384]{1,0:T(8,128)S(1)}, u32[]{:S(2)}, u32[]{:S(2)}) collective-permute-start(f32[64,384]{1,0:T(8,128)S(1)} %get-tuple-element.22), channel_id=1, source_target_pairs={{0,0},{1,16},{2,2},{3,18},{4,4},{5,20},{6,6},{7,22},{8,8},{9,24},{... | collective-permute-start | bytes 294920 | tf_op jit(solution)/shard_map/ppermute | solution.py:211
  123.8 2.6 %collective-permute-start.9 = (f32[64,384]{1,0:T(8,128)S(1)}, f32[64,384]{1,0:T(8,128)S(1)}, u32[]{:S(2)}, u32[]{:S(2)}) collective-permute-start(f32[64,384]{1,0:T(8,128)S(1)} %get-tuple-element.21), channel_id=1, source_target_pairs={{0,16},{1,0},{2,18},{3,2},{4,20},{5,4},{6,22},{7,6},{8,24},{9,8},{... | collective-permute-start | bytes 294920 | tf_op jit(solution)/shard_map/ppermute | solution.py:212

commit v3 on v1

--- a/solution.py
+++ b/solution.py
@@ -10,8 +10,11 @@
 YS, ZS = 4, 8
 STEP = {"x": (1, 0), "U": (0, 1), "D": (0, -1)}
 SLICES = ((64, (0, 0, 0, 1, 1, 2, 4), "DUxxDxD", "xUDUDUU"),)
+UNITS = 32767.0
+SMALLEST = 2.0**-126
+LAST_DEPTH = 2048
 DEPTH = 2048
-GROUPS = (((0, 4), (4, 7), (7, 8)),)
+GROUPS = (((0, 4), (4, 6), (6, 8)),)
 ORDER = (
     ("s00", ()), ("s01", ()), ("s02", ()), ("s03", ("own",)), ("s04", ("s00",)), ("s05", ("s01",)),
     ("m00", ()), ("s06", ("m00",)), ("m01", ()), ("m02", ("m01",)),
@@ -65,6 +68,7 @@
         in_specs=[pl.BlockSpec((rows, DEPTH), lambda k: (0, k))],
         out_specs=pl.BlockSpec((DEPTH, rows), lambda k: (k, 0)),
         out_shape=jax.ShapeDtypeStruct((depth, rows), amplitudes.dtype),
+        compiler_params=pltpu.CompilerParams(vmem_limit_bytes=8 * 1024 * 1024),
         cost_estimate=pl.CostEstimate(flops=0, bytes_accessed=0, transcendentals=0),
     )(amplitudes)
 
@@ -91,56 +95,124 @@
     accumulate(total, blocks, (own, other))
 
 
+def coded(sums):
+    largest = jnp.maximum(jnp.max(jnp.abs(sums), axis=1, keepdims=True), SMALLEST)
+    power = jnp.clip(jnp.floor(jnp.log2(largest)) + 1.0, -126.0, 126.0)
+    scale = jnp.exp2(-power)
+    part = jnp.ceil(largest * scale * 256.0)
+    whole = jnp.round(sums * scale * (256.0 * UNITS / part))
+    place = lax.broadcasted_iota(jnp.int32, (16, 128), 1)
+    note = jnp.zeros((16, 128), jnp.float32)
+    pieces = []
+    for g in range(sums.shape[0] // 16):
+        these = slice(g * 16, (g + 1) * 16)
+        note = jnp.where(place == 2 * g, power[these], jnp.where(place == 2 * g + 1, part[these], note))
+        pieces.append(whole[these])
+    return jnp.concatenate([*pieces, note], axis=1).astype(jnp.int32).astype(jnp.int16)
+
+
+def coded_shape(rows, width):
+    return (16, rows // 16 * width + 128)
+
+
+def decoded(share, width):
+    count = share.shape[1] // width
+    rows = []
+    for g in range(count):
+        note = share[:, count * width :].astype(jnp.float32)
+        power, part = note[:, 2 * g : 2 * g + 1], note[:, 2 * g + 1 : 2 * g + 2]
+        scale = part * (1.0 / (256.0 * UNITS)) * jnp.exp2(power)
+        rows.append(share[:, g * width : (g + 1) * width].astype(jnp.float32) * scale)
+    return jnp.concatenate(rows, axis=0)
+
+
 def finish_kernel(counts, spots, *refs):
     last = counts[-1]
-    blocks, (own, other) = refs[:last], refs[last : last + 2]
-    earlier, out, total = refs[last + 2 : -2], refs[-2], refs[-1]
+    blocks, (own, other), earlier = refs[:last], refs[last : last + 2], refs[last + 2 : -6]
+    kept, up, down, far, total, ordered = refs[-6:]
     accumulate(total, blocks, (own, other))
 
     @pl.when(pl.program_id(0) == pl.num_programs(0) - 1)
     def _():
-        row = lax.axis_index("row")
+        row, z = lax.axis_index("row"), lax.axis_index("col") // 2
         x, y, core = row // (2 * YS), row // 2 % YS, row % 2
-        n = out.shape[1]
+        n = ordered.shape[1]
         i = 0
         for count, sums in zip(counts, (*earlier, total)):
             for j in range(count):
                 (x0, y0), (x1, y1) = spots[0][i], spots[1][i]
                 from_x = jnp.where(core == 0, x ^ x0, x ^ x1)
                 from_y = jnp.where(core == 0, (y + YS - y0) % YS, (y + YS - y1) % YS)
-                out[from_x * YS + from_y] = sums[j * n : (j + 1) * n, :]
+                ordered[(from_x * YS + from_y + ZS - z) % ZS] = sums[j * n : (j + 1) * n, :]
                 i += 1
-
-
-def multiply(kernel, blocks, own, other, earlier, out_shape, scratch):
+        for place, step in enumerate((0, 2, 6)):
+            kept[place] = ordered[step]
+        up[0], up[1] = coded(ordered[1]), coded(ordered[3])
+        down[0], down[1] = coded(ordered[7]), coded(ordered[5])
+        far[...] = coded(ordered[4])
+
+
+def pass_kernel(kept, from_below, from_above, from_far, up, down):
+    width = kept.shape[2]
+    even = (lax.axis_index("col") // 2) % 2 == 0
+    far = decoded(from_far[...], width)
+    up[...] = coded(kept[1] + decoded(from_below[1], width) + jnp.where(even, far, 0.0))
+    down[...] = coded(kept[2] + decoded(from_above[1], width) + jnp.where(even, 0.0, far))
+
+
+def along_z(sums, even, odd):
+    pairs = [(a * 2 + b, (a + (odd if a % 2 else even)) % ZS * 2 + b) for a in range(ZS) for b in range(2)]
+    return lax.ppermute(sums, "col", pairs)
+
+
+def sum_along_z(kept, up, down, far):
+    _, n, width = kept.shape
+    from_far = along_z(far, 2, -2)
+    from_below, from_above = along_z(up, 1, 1), along_z(down, -1, -1)
+    shape = jax.ShapeDtypeStruct(coded_shape(n, width), jnp.int16)
+    up, down = pl.pallas_call(
+        pass_kernel,
+        out_shape=[shape, shape],
+        compiler_params=pltpu.CompilerParams(vmem_limit_bytes=12 * 1024 * 1024),
+        cost_estimate=pl.CostEstimate(flops=0, bytes_accessed=0, transcendentals=0),
+    )(kept, from_below, from_above, from_far)
+    near = (from_below[0], from_above[0], along_z(up, 2, 2), along_z(down, -2, -2))
+    return kept[0] + sum(decoded(share, width) for share in near)
+
+
+def multiply(kernel, blocks, own, other, earlier, outs, scratch, step=DEPTH, room=16):
     n, depth = blocks[0].shape
     rows = own.shape[1]
     whole = lambda shape: pl.BlockSpec(shape, lambda k: (0,) * len(shape))
     return pl.pallas_call(
         kernel,
-        grid=(depth // DEPTH,),
-        in_specs=[pl.BlockSpec((n, DEPTH), lambda k: (0, k))] * len(blocks)
-        + [pl.BlockSpec((DEPTH, rows), lambda k: (k, 0))] * 2
+        grid=(depth // step,),
+        in_specs=[pl.BlockSpec((n, step), lambda k: (0, k))] * len(blocks)
+        + [pl.BlockSpec((step, rows), lambda k: (k, 0))] * 2
         + [whole(sums.shape) for sums in earlier],
-        out_specs=whole(out_shape),
-        out_shape=jax.ShapeDtypeStruct(out_shape, jnp.float32),
+        out_specs=[whole(out.shape) for out in outs],
+        out_shape=list(outs),
         scratch_shapes=scratch,
-        compiler_params=pltpu.CompilerParams(vmem_limit_bytes=16 * 1024 * 1024),
+        compiler_params=pltpu.CompilerParams(vmem_limit_bytes=room * 1024 * 1024),
         cost_estimate=pl.CostEstimate(flops=0, bytes_accessed=0, transcendentals=0),
     )(*blocks, own, other, *earlier)
 
 
 def sums_of(blocks, own, other):
     n, width = blocks[0].shape[0], 2 * own.shape[1]
-    return multiply(product_kernel, blocks, own, other, (), (len(blocks) * n, width), ())
+    out = jax.ShapeDtypeStruct((len(blocks) * n, width), jnp.float32)
+    return multiply(product_kernel, blocks, own, other, (), (out,), ())[0]
 
 
 def last_sums(blocks, own, other, earlier, spots, groups):
     n, width = blocks[0].shape[0], 2 * own.shape[1]
     counts = tuple(b - a for a, b in groups)
     kernel = functools.partial(finish_kernel, counts, spots)
-    scratch = [pltpu.VMEM((len(blocks) * n, width), jnp.float32)]
-    return multiply(kernel, blocks, own, other, earlier, (8, n, width), scratch)
+    scratch = [pltpu.VMEM((len(blocks) * n, width), jnp.float32), pltpu.VMEM((8, n, width), jnp.float32)]
+    one = coded_shape(n, width)
+    pair = jax.ShapeDtypeStruct((2, *one), jnp.int16)
+    outs = (jax.ShapeDtypeStruct((3, n, width), jnp.float32), pair, pair, jax.ShapeDtypeStruct(one, jnp.int16))
+    return multiply(kernel, blocks, own, other, earlier, outs, scratch, LAST_DEPTH, 18)
 
 
 def after(value, *others):
@@ -171,7 +243,7 @@
         else:
             spots = (places(sources, first), places(sources, second))
             done[name] = last_sums(blocks, done["own"], done["other"], earlier[s], spots, GROUPS[s])
-            yield done[name]
+            return done[name]
 
 
 def on_device(amplitudes, integrals, pair_first, pair_second, occ_energy, vir_energy):
@@ -179,18 +251,11 @@
     row, col = lax.axis_index("row"), lax.axis_index("col")
     core, h = row % 2, col % 2
     same = h == core
-    along_z = [[z * 2 + b for z in range(ZS)] for b in range(2)]
-    done = []
-    for sums in partials(integrals.T, amplitudes):
-        if done:
-            sums = after(sums, shares)
-        shares = lax.all_to_all(sums, "col", split_axis=0, concat_axis=0, tiled=True, axis_index_groups=along_z)
-        mine = jnp.sum(shares, axis=0)
-        own, theirs = mine[:, :local_rows], mine[:, local_rows:]
-        a = lax.ppermute(jnp.where(same, own, theirs), ("row", "col"), swap_perm(0))
-        b = lax.ppermute(jnp.where(same, theirs, own), ("row", "col"), swap_perm(1))
-        done.append(a + b)
-    ladder = jnp.concatenate(done, axis=0)
+    mine = sum_along_z(*partials(integrals.T, amplitudes))
+    own, theirs = mine[:, :local_rows], mine[:, local_rows:]
+    ladder = lax.ppermute(jnp.where(same, own, theirs), ("row", "col"), swap_perm(0)) + lax.ppermute(
+        jnp.where(same, theirs, own), ("row", "col"), swap_perm(1)
+    )
 
     nocc_count = occ_energy.shape[0]
     pair_rows = row * local_rows + jnp.arange(local_rows, dtype=jnp.int32)

time: 141 us -> 117 us (0.83)
  Pallas kernels: 40 us -> 27.7 us
  waiting for transfers between devices: 64.6 us -> 52.4 us
  starting transfers between devices: 26.6 us -> 22.9 us
  local copies, waits for them, and re-layouts: 7.8 us -> 9.76 us
    all_to_all x1 -> x0, waiting for transfers between devices: 36.8 us -> none  [on_device(): lax.all_to_all(sums, 'col', split_axis=0, concat_axis=0, tiled=True, axis...]
    ppermute x7, waiting for transfers between devices: 25.5 us -> 38.3 us  [partials(): done[name] = lax.ppermute(block, 'row', row_perm((first[i], second[i])))]
    pallas_call x2, Pallas kernels: 18.2 us -> 5.76 us  [turned(): pl.pallas_call(turn_kernel, grid=(depth // DEPTH,), in_specs=[pl.BlockSpe...]
    ppermute x2 -> x7, waiting for transfers between devices: 2.21 us -> 14 us  [the longest x5 11.8 us: along_z(): return lax.ppermute(sums, 'col', pairs)]
    all_to_all x1 -> x0, starting transfers between devices: 8.25 us -> none  [on_device(): lax.all_to_all(sums, 'col', split_axis=0, concat_axis=0, tiled=True, axis...]
    ppermute x2 -> x7, starting transfers between devices: 7.99 us -> 14.3 us  [the longest x5 7.56 us: along_z(): return lax.ppermute(sums, 'col', pairs)]
    unnamed x14 -> x22, local copies, waits for them, and re-layouts: 7.8 us -> 9.74 us
    ppermute x7, starting transfers between devices: 7.16 us -> 5.36 us  [partials(): done[name] = lax.ppermute(block, 'row', row_perm((first[i], second[i])))]
  transfers between devices with their start and end apart: 11 -> 15, of which waited for: 6 -> 9; matrix products, arithmetic and copies ran while one was open for 0% -> 1% of each run, Pallas kernels for 24% -> 18%
where the time goes in v3:
time: 117 us; the launch traced here: 116 us
  waiting for transfers between devices  52.4 us (45%)
  Pallas kernels  27.7 us (24%)
  starting transfers between devices  22.9 us (20%)
  local copies, waits for them, and re-layouts  9.76 us (8%)
  other arithmetic  2.48 us (2%)
    ppermute x7, waiting for transfers between devices, partials(): done[name] = lax.ppermute(block, 'row', row_perm((first[i], second[i])))  38.3 us
    pallas_call x3, Pallas kernels, multiply(): pl.pallas_call(kernel, grid=(depth // step,), in_specs=[pl.BlockSpec((n,...  21.6 us
    ppermute x5, waiting for transfers between devices, along_z(): return lax.ppermute(sums, 'col', pairs)  11.8 us
    unnamed x22, local copies, waits for them, and re-layouts  9.74 us
    ppermute x5, starting transfers between devices, along_z(): return lax.ppermute(sums, 'col', pairs)  7.56 us
    ppermute x1, starting transfers between devices, on_device(): lax.ppermute(jnp.where(same, own, theirs), ('row', 'col'), swap_perm(0))  6.69 us
    pallas_call x2, Pallas kernels, turned(): pl.pallas_call(turn_kernel, grid=(depth // DEPTH,), in_specs=[pl.BlockSpe...  5.76 us
    ppermute x7, starting transfers between devices, partials(): done[name] = lax.ppermute(block, 'row', row_perm((first[i], second[i])))  5.36 us
  transfers between devices with their start and end apart: 15, of which 9 were waited for; matrix products, arithmetic and copies ran while one was open for 1% of the time, Pallas kernels for 18%

profile of v3, /device:TPU:1, one launch (start us, length us, event | category | flops | bytes accessed | tf_op | source)
XLA Modules:
  0.0 115.5 jit_solution(11776879973321597126)
XLA Ops:
  0.0 3.2 %collective-permute-start.5 = (bf16[384,10240]{1,0:T(8,128)(2,1)}, bf16[384,10240]{1,0:T(8,128)(2,1)S(1)}, u32[]{:S(2)}, u32[]{:S(2)}) collective-permute-start(bf16[384,10240]{1,0:T(8,128)(2,1)} %rows.1), channel_id=1, source_target_pairs={{0,16},{16,0},{32,48},{48,32},{64,80},{80,64},{96,112},{112,96},{1... | collective-permute-start | bytes 23592968 | tf_op jit(solution)/shard_map/ppermute | solution.py:223
  3.2 0.0 collective-permute-start.2
  3.2 0.8 collective-permute-start
  4.0 1.9 %collective-permute-start.6 = (bf16[64,10240]{1,0:T(8,128)(2,1)}, bf16[64,10240]{1,0:T(8,128)(2,1)S(1)}, u32[]{:S(2)}, u32[]{:S(2)}) collective-permute-start(bf16[64,10240]{1,0:T(8,128)(2,1)} %bitcast.11), channel_id=1, source_target_pairs={{0,128},{16,112},{32,160},{48,16},{64,192},{80,48},{96,224},{112,8... | collective-permute-start | bytes 3932168 | tf_op jit(solution)/shard_map/ppermute | solution.py:234
  5.9 3.2 %copy-done.5 = bf16[384,10240]{1,0:T(8,128)(2,1)S(1)} copy-done((bf16[384,10240]{1,0:T(8,128)(2,1)S(1)}, bf16[384,10240]{1,0:T(8,128)(2,1)}, u32[]{:S(2)}) %copy-start.5) | copy-done | bytes 7864344
  9.2 2.9 %shard_map.64.refs_2_.refs_4_ = bf16[10240,384]{1,0:T(8,128)(2,1)S(1)} custom-call(bf16[384,10240]{1,0:T(8,128)(2,1)S(1)} %copy-done.5), custom_call_target="tpu_custom_call" | custom-call | tf_op jit(solution)/shard_map/pallas_call | solution.py:65
  12.0 0.0 copy-start
  12.0 0.0 copy-start.6
  12.1 19.7 %collective-permute-done.2.refs_1_ = bf16[64,10240]{1,0:T(8,128)(2,1)} collective-permute-done((bf16[64,10240]{1,0:T(8,128)(2,1)}, bf16[64,10240]{1,0:T(8,128)(2,1)}, u32[]{:S(2)}, u32[]{:S(2)}) %collective-permute-start.2) | collective-permute-done | bytes 1310752 | tf_op jit(solution)/shard_map/ppermute | solution.py:234
  31.8 0.0 collective-permute-start.3
  31.8 2.7 %collective-permute-start.4 = (bf16[64,10240]{1,0:T(8,128)(2,1)}, bf16[64,10240]{1,0:T(8,128)(2,1)}, u32[]{:S(2)}, u32[]{:S(2)}) collective-permute-start(bf16[64,10240]{1,0:T(8,128)(2,1)} %collective-permute-done.2.refs_1_), channel_id=1, source_target_pairs={{0,96},{16,112},{32,0},{48,16},{64,32},{80,48},{96,64},{112,80},{1... | collective-permute-start | bytes 3932168 | tf_op jit(solution)/shard_map/ppermute | solution.py:234
  34.5 0.0 collective-permute-done.refs_2_
  34.5 0.0 collective-permute-start.1
  34.5 0.0 collective-permute-done.5.rows
  34.5 2.9 %shard_map.65.refs_3_.refs_5_ = bf16[10240,384]{1,0:T(8,128)(2,1)S(1)} custom-call(bf16[384,10240]{1,0:T(8,128)(2,1)S(1)} %collective-permute-done.5.rows), custom_call_target="tpu_custom_call" | custom-call | tf_op jit(solution)/shard_map/pallas_call | solution.py:65
  37.4 0.0 copy-start.3
  37.4 0.0 collective-permute-done.6.refs_3_
  37.4 0.0 copy-done
  37.4 0.0 copy-done.6
  37.4 9.2 %shard_map.67.refs_4_ = f32[256,768]{1,0:T(8,128)S(1)} custom-call(bf16[64,10240]{1,0:T(8,128)(2,1)S(1)} %bitcast.12, bf16[64,10240]{1,0:T(8,128)(2,1)} %collective-permute-done.2.refs_1_, bf16[64,10240]{1,0:T(8,128)(2,1)} %collective-permute-done.refs_2_, bf16[64,10240]{1,0:T(8,128)(2,1)S(1)} %collective-permute-done.6.refs_3_, ...), custom_call_target="tpu_custom_call" | custom-call | tf_op jit(solution)/shard_map/pallas_call | solution.py:187
  46.6 0.0 copy-done.3
  46.6 3.1 %collective-permute-done.3.refs_0_ = bf16[64,10240]{1,0:T(8,128)(2,1)S(1)} collective-permute-done((bf16[64,10240]{1,0:T(8,128)(2,1)}, bf16[64,10240]{1,0:T(8,128)(2,1)S(1)}, u32[]{:S(2)}, u32[]{:S(2)}) %collective-permute-start.3) | collective-permute-done | bytes 1310752 | tf_op jit(solution)/shard_map/ppermute | solution.py:234
  49.7 0.0 collective-permute-start.7
  49.7 10.3 %collective-permute-done.4.refs_1_ = bf16[64,10240]{1,0:T(8,128)(2,1)} collective-permute-done((bf16[64,10240]{1,0:T(8,128)(2,1)}, bf16[64,10240]{1,0:T(8,128)(2,1)}, u32[]{:S(2)}, u32[]{:S(2)}) %collective-permute-start.4) | collective-permute-done | bytes 1310752 | tf_op jit(solution)/shard_map/ppermute | solution.py:234
  60.0 3.2 %copy-done.1 = bf16[10240,384]{1,0:T(8,128)(2,1)S(1)} copy-done((bf16[10240,384]{1,0:T(8,128)(2,1)S(1)}, bf16[10240,384]{1,0:T(8,128)(2,1)}, u32[]{:S(2)}) %copy-start.1) | copy-done | bytes 7864344
  63.2 3.2 %copy-done.4 = bf16[10240,384]{1,0:T(8,128)(2,1)S(1)} copy-done((bf16[10240,384]{1,0:T(8,128)(2,1)S(1)}, bf16[10240,384]{1,0:T(8,128)(2,1)}, u32[]{:S(2)}) %copy-start.4) | copy-done | bytes 7864344
  66.4 6.2 %shard_map.66.refs_5_ = f32[128,768]{1,0:T(8,128)S(1)} custom-call(bf16[64,10240]{1,0:T(8,128)(2,1)S(1)} %collective-permute-done.3.refs_0_, bf16[64,10240]{1,0:T(8,128)(2,1)} %collective-permute-done.4.refs_1_, bf16[10240,384]{1,0:T(8,128)(2,1)S(1)} %copy-done.1, bf16[10240,384]{1,0:T(8,128)(2,1)S(1)} %copy-done.4), custom_call_target="tpu_custom_call" | custom-call | tf_op jit(solution)/shard_map/pallas_call | solution.py:187
  72.6 0.0 copy-start.8
  72.6 0.0 collective-permute-done.1.refs_0_
  72.6 5.2 %collective-permute-done.7.refs_1_ = bf16[64,10240]{1,0:T(8,128)(2,1)} collective-permute-done((bf16[64,10240]{1,0:T(8,128)(2,1)S(1)}, bf16[64,10240]{1,0:T(8,128)(2,1)}, u32[]{:S(2)}, u32[]{:S(2)}) %collective-permute-start.7) | collective-permute-done | bytes 1310752 | tf_op jit(solution)/shard_map/ppermute | solution.py:234
  77.9 0.0 copy-done.2
  77.9 6.2 %shard_map.68 = (f32[3,64,768]{2,1,0:T(8,128)S(1)}, s16[2,16,3200]{2,1,0:T(8,128)(2,1)S(1)}, s16[2,16,3200]{2,1,0:T(8,128)(2,1)S(1)}, s16[16,3200]{1,0:T(8,128)(2,1)S(1)}) custom-call(bf16[64,10240]{1,0:T(8,128)(2,1)S(1)} %collective-permute-done.1.refs_0_, bf16[64,10240]{1,0:T(8,128)(2,1)} %collective-permute-done.7.refs_1_, ...), custom_call_target="tpu_custom_call" | custom-call | tf_op jit(solution)/shard_map/pallas_call | solution.py:187
  84.1 0.8 collective-permute-start.8
  84.9 4.2 %collective-permute-start.9 = (s16[2,16,3200]{2,1,0:T(8,128)(2,1)S(1)}, s16[2,16,3200]{2,1,0:T(8,128)(2,1)S(1)}, u32[]{:S(2)}, u32[]{:S(2)}) collective-permute-start(s16[2,16,3200]{2,1,0:T(8,128)(2,1)S(1)} %get-tuple-element.23), channel_id=1, source_target_pairs={{0,14},{1,15},{2,0},{3,1},{4,2},{5,3},{6,4},{7,5},{8,6},{9,7},{10,... | collective-permute-start | bytes 614408 | tf_op jit(solution)/shard_map/ppermute | solution.py:165
  89.2 0.1 collective-permute-start.10
  89.2 0.0 copy-done.8
  89.3 0.2 select_reduce_fusion.2
  89.4 8.1 %collective-permute-done.10.from_far = s16[16,3200]{1,0:T(8,128)(2,1)S(1)} collective-permute-done((s16[16,3200]{1,0:T(8,128)(2,1)S(1)}, s16[16,3200]{1,0:T(8,128)(2,1)S(1)}, u32[]{:S(2)}, u32[]{:S(2)}) %collective-permute-start.10) | collective-permute-done | bytes 102432 | tf_op jit(solution)/shard_map/ppermute | solution.py:165
  97.6 0.0 collective-permute-done.8.from_below
  97.6 0.0 collective-permute-done.9.from_above
  97.6 0.3 shard_map.69
  97.9 1.2 %collective-permute-start.12 = (s16[16,3200]{1,0:T(8,128)(2,1)S(1)}, s16[16,3200]{1,0:T(8,128)(2,1)S(1)}, u32[]{:S(2)}, u32[]{:S(2)}) collective-permute-start(s16[16,3200]{1,0:T(8,128)(2,1)S(1)} %get-tuple-element.26), channel_id=1, source_target_pairs={{0,12},{1,13},{2,14},{3,15},{4,0},{5,1},{6,2},{7,3},{8,4},{9,5},{1... | collective-permute-start | bytes 307208 | tf_op jit(solution)/shard_map/ppermute | solution.py:165
  99.1 1.2 %collective-permute-start.11 = (s16[16,3200]{1,0:T(8,128)(2,1)S(1)}, s16[16,3200]{1,0:T(8,128)(2,1)S(1)}, u32[]{:S(2)}, u32[]{:S(2)}) collective-permute-start(s16[16,3200]{1,0:T(8,128)(2,1)S(1)} %get-tuple-element.25), channel_id=1, source_target_pairs={{0,4},{1,5},{2,6},{3,7},{4,8},{5,9},{6,10},{7,11},{8,12},{9,13},{1... | collective-permute-start | bytes 307208 | tf_op jit(solution)/shard_map/ppermute | solution.py:165
  100.4 0.2 fusion.39
  100.6 0.2 fusion.51
  100.9 0.1 convert_multiply_fusion.11
  101.0 0.0 copy-start.7
  101.0 0.0 copy-start.9
  101.0 0.0 copy-start.10
  101.0 0.1 convert_multiply_fusion.15
  101.1 1.8 %collective-permute-done.12 = s16[16,3200]{1,0:T(8,128)(2,1)S(1)} collective-permute-done((s16[16,3200]{1,0:T(8,128)(2,1)S(1)}, s16[16,3200]{1,0:T(8,128)(2,1)S(1)}, u32[]{:S(2)}, u32[]{:S(2)}) %collective-permute-start.12) | collective-permute-done | bytes 102432 | tf_op jit(solution)/shard_map/ppermute | solution.py:165
  102.9 0.2 fusion.15
  103.1 1.9 %collective-permute-done.11 = s16[16,3200]{1,0:T(8,128)(2,1)S(1)} collective-permute-done((s16[16,3200]{1,0:T(8,128)(2,1)S(1)}, s16[16,3200]{1,0:T(8,128)(2,1)S(1)}, u32[]{:S(2)}, u32[]{:S(2)}) %collective-permute-start.11) | collective-permute-done | bytes 102432 | tf_op jit(solution)/shard_map/ppermute | solution.py:165
  105.0 0.2 fusion.27
  105.2 0.1 convert_multiply_fusion.3
  105.3 0.1 convert_multiply_fusion.7
  105.4 0.1 fusion.2
  105.5 6.7 %collective-permute-start.13 = (f32[64,384]{1,0:T(8,128)S(1)}, f32[64,384]{1,0:T(8,128)S(1)}, u32[]{:S(2)}, u32[]{:S(2)}) collective-permute-start(f32[64,384]{1,0:T(8,128)S(1)} %get-tuple-element.48), channel_id=1, source_target_pairs={{0,0},{1,16},{2,2},{3,18},{4,4},{5,20},{6,6},{7,22},{8,8},{9,24},{... | collective-permute-start | bytes 294920 | tf_op jit(solution)/shard_map/ppermute | solution.py:256
  112.2 0.1 collective-permute-start.14
  112.3 0.0 copy-done.7
  112.3 0.3 select_reduce_fusion.1
  112.6 1.9 %collective-permute-done.13 = f32[64,384]{1,0:T(8,128)S(1)} collective-permute-done((f32[64,384]{1,0:T(8,128)S(1)}, f32[64,384]{1,0:T(8,128)S(1)}, u32[]{:S(2)}, u32[]{:S(2)}) %collective-permute-start.13) | collective-permute-done | bytes 98336 | tf_op jit(solution)/shard_map/ppermute | solution.py:256
  114.5 0.3 collective-permute-done.14
  114.8 0.7 fusion.3
  (15 shorter events, 0.1 us)
Async XLA Ops:
  0.0 34.5 %collective-permute-start.5 = (bf16[384,10240]{1,0:T(8,128)(2,1)}, bf16[384,10240]{1,0:T(8,128)(2,1)S(1)}, u32[]{:S(2)}, u32[]{:S(2)}) collective-permute-start(bf16[384,10240]{1,0:T(8,128)(2,1)} %rows.1), channel_id=1, source_target_pairs={{0,16},{16,0},{32,48},{48,32},{64,80},{80,64},{96,112},{112,96},{1... | collective-permute-start | bytes 23592968 | tf_op jit(solution)/shard_map/ppermute | solution.py:223
  3.2 28.6 %collective-permute-start.2 = (bf16[64,10240]{1,0:T(8,128)(2,1)}, bf16[64,10240]{1,0:T(8,128)(2,1)}, u32[]{:S(2)}, u32[]{:S(2)}) collective-permute-start(bf16[64,10240]{1,0:T(8,128)(2,1)} %bitcast.9), channel_id=1, source_target_pairs={{0,96},{16,144},{32,0},{48,176},{64,32},{80,208},{96,64},{112,240}... | collective-permute-start | bytes 3932168 | tf_op jit(solution)/shard_map/ppermute | solution.py:234
  3.2 31.2 %collective-permute-start = (bf16[64,10240]{1,0:T(8,128)(2,1)}, bf16[64,10240]{1,0:T(8,128)(2,1)}, u32[]{:S(2)}, u32[]{:S(2)}) collective-permute-start(bf16[64,10240]{1,0:T(8,128)(2,1)} %bitcast.10), channel_id=1, source_target_pairs={{0,32},{16,48},{32,64},{48,80},{64,96},{80,112},{96,0},{112,16},{1... | collective-permute-start | bytes 3932168 | tf_op jit(solution)/shard_map/ppermute | solution.py:234
  4.0 33.4 %collective-permute-start.6 = (bf16[64,10240]{1,0:T(8,128)(2,1)}, bf16[64,10240]{1,0:T(8,128)(2,1)S(1)}, u32[]{:S(2)}, u32[]{:S(2)}) collective-permute-start(bf16[64,10240]{1,0:T(8,128)(2,1)} %bitcast.11), channel_id=1, source_target_pairs={{0,128},{16,112},{32,160},{48,16},{64,192},{80,48},{96,224},{112,8... | collective-permute-start | bytes 3932168 | tf_op jit(solution)/shard_map/ppermute | solution.py:234
  5.9 3.2 %copy-start.5 = (bf16[384,10240]{1,0:T(8,128)(2,1)S(1)}, bf16[384,10240]{1,0:T(8,128)(2,1)}, u32[]{:S(2)}) copy-start(bf16[384,10240]{1,0:T(8,128)(2,1)} %rows.1) | copy-start | bytes 23592964
  12.0 25.4 %copy-start = (bf16[10240,384]{1,0:T(8,128)(2,1)}, bf16[10240,384]{1,0:T(8,128)(2,1)S(1)}, u32[]{:S(2)}) copy-start(bf16[10240,384]{1,0:T(8,128)(2,1)S(1)} %shard_map.64.refs_2_.refs_4_) | copy-start | bytes 23592964
  12.0 25.4 %copy-start.6 = (bf16[10240,64]{0,1:T(8,128)(2,1)S(1)}, bf16[10240,64]{0,1:T(8,128)(2,1)}, u32[]{:S(2)}) copy-start(bf16[10240,64]{0,1:T(8,128)(2,1)} %param.7) | copy-start | bytes 3932164
  31.8 17.9 %collective-permute-start.3 = (bf16[64,10240]{1,0:T(8,128)(2,1)}, bf16[64,10240]{1,0:T(8,128)(2,1)S(1)}, u32[]{:S(2)}, u32[]{:S(2)}) collective-permute-start(bf16[64,10240]{1,0:T(8,128)(2,1)} %collective-permute-done.2.refs_1_), channel_id=1, source_target_pairs={{0,128},{16,48},{32,160},{48,80},{64,192},{80,112},{96,224},{112,1... | collective-permute-start | bytes 3932168 | tf_op jit(solution)/shard_map/ppermute | solution.py:234
  31.8 28.2 %collective-permute-start.4 = (bf16[64,10240]{1,0:T(8,128)(2,1)}, bf16[64,10240]{1,0:T(8,128)(2,1)}, u32[]{:S(2)}, u32[]{:S(2)}) collective-permute-start(bf16[64,10240]{1,0:T(8,128)(2,1)} %collective-permute-done.2.refs_1_), channel_id=1, source_target_pairs={{0,96},{16,112},{32,0},{48,16},{64,32},{80,48},{96,64},{112,80},{1... | collective-permute-start | bytes 3932168 | tf_op jit(solution)/shard_map/ppermute | solution.py:234
  34.5 38.2 %collective-permute-start.1 = (bf16[64,10240]{1,0:T(8,128)(2,1)}, bf16[64,10240]{1,0:T(8,128)(2,1)S(1)}, u32[]{:S(2)}, u32[]{:S(2)}) collective-permute-start(bf16[64,10240]{1,0:T(8,128)(2,1)} %collective-permute-done.refs_2_), channel_id=1, source_target_pairs={{0,128},{16,48},{32,160},{48,80},{64,192},{80,112},{96,224},{112,1... | collective-permute-start | bytes 3932168 | tf_op jit(solution)/shard_map/ppermute | solution.py:234
  37.4 9.2 %copy-start.3 = (bf16[10240,384]{1,0:T(8,128)(2,1)}, bf16[10240,384]{1,0:T(8,128)(2,1)S(1)}, u32[]{:S(2)}) copy-start(bf16[10240,384]{1,0:T(8,128)(2,1)S(1)} %shard_map.65.refs_3_.refs_5_) | copy-start | bytes 23592964
  49.7 28.2 %collective-permute-start.7 = (bf16[64,10240]{1,0:T(8,128)(2,1)S(1)}, bf16[64,10240]{1,0:T(8,128)(2,1)}, u32[]{:S(2)}, u32[]{:S(2)}) collective-permute-start(bf16[64,10240]{1,0:T(8,128)(2,1)S(1)} %collective-permute-done.3.refs_0_), channel_id=1, source_target_pairs={{0,96},{16,48},{32,0},{48,80},{64,32},{80,112},{96,64},{112,16},{1... | collective-permute-start | bytes 3932168 | tf_op jit(solution)/shard_map/ppermute | solution.py:234
  60.0 3.2 %copy-start.1 = (bf16[10240,384]{1,0:T(8,128)(2,1)S(1)}, bf16[10240,384]{1,0:T(8,128)(2,1)}, u32[]{:S(2)}) copy-start(bf16[10240,384]{1,0:T(8,128)(2,1)} %copy-done) | copy-start | bytes 23592964
  63.2 3.2 %copy-start.4 = (bf16[10240,384]{1,0:T(8,128)(2,1)S(1)}, bf16[10240,384]{1,0:T(8,128)(2,1)}, u32[]{:S(2)}) copy-start(bf16[10240,384]{1,0:T(8,128)(2,1)} %copy-done.3) | copy-start | bytes 23592964
  66.4 11.4 %copy-start.2 = (bf16[10240,384]{1,0:T(8,128)(2,1)S(1)}, bf16[10240,384]{1,0:T(8,128)(2,1)}, u32[]{:S(2)}) copy-start(bf16[10240,384]{1,0:T(8,128)(2,1)} %copy-done) | copy-start | bytes 23592964
  72.6 16.6 %copy-start.8 = (f32[200]{0:T(256)S(1)}, f32[200]{0:T(256)}, u32[]{:S(2)}) copy-start(f32[200]{0:T(256)} %param.10) | copy-start | bytes 2404
  84.1 13.5 %collective-permute-start.8 = (s16[2,16,3200]{2,1,0:T(8,128)(2,1)S(1)}, s16[2,16,3200]{2,1,0:T(8,128)(2,1)S(1)}, u32[]{:S(2)}, u32[]{:S(2)}) collective-permute-start(s16[2,16,3200]{2,1,0:T(8,128)(2,1)S(1)} %get-tuple-element.22), channel_id=1, source_target_pairs={{0,2},{1,3},{2,4},{3,5},{4,6},{5,7},{6,8},{7,9},{8,10},{9,11},{10,... | collective-permute-start | bytes 614408 | tf_op jit(solution)/shard_map/ppermute | solution.py:165
  84.9 12.7 %collective-permute-start.9 = (s16[2,16,3200]{2,1,0:T(8,128)(2,1)S(1)}, s16[2,16,3200]{2,1,0:T(8,128)(2,1)S(1)}, u32[]{:S(2)}, u32[]{:S(2)}) collective-permute-start(s16[2,16,3200]{2,1,0:T(8,128)(2,1)S(1)} %get-tuple-element.23), channel_id=1, source_target_pairs={{0,14},{1,15},{2,0},{3,1},{4,2},{5,3},{6,4},{7,5},{8,6},{9,7},{10,... | collective-permute-start | bytes 614408 | tf_op jit(solution)/shard_map/ppermute | solution.py:165
  89.2 8.4 %collective-permute-start.10 = (s16[16,3200]{1,0:T(8,128)(2,1)S(1)}, s16[16,3200]{1,0:T(8,128)(2,1)S(1)}, u32[]{:S(2)}, u32[]{:S(2)}) collective-permute-start(s16[16,3200]{1,0:T(8,128)(2,1)S(1)} %get-tuple-element.24), channel_id=1, source_target_pairs={{0,4},{1,5},{2,14},{3,15},{4,8},{5,9},{6,2},{7,3},{8,12},{9,13},{1... | collective-permute-start | bytes 307208 | tf_op jit(solution)/shard_map/ppermute | solution.py:165
  97.9 4.9 %collective-permute-start.12 = (s16[16,3200]{1,0:T(8,128)(2,1)S(1)}, s16[16,3200]{1,0:T(8,128)(2,1)S(1)}, u32[]{:S(2)}, u32[]{:S(2)}) collective-permute-start(s16[16,3200]{1,0:T(8,128)(2,1)S(1)} %get-tuple-element.26), channel_id=1, source_target_pairs={{0,12},{1,13},{2,14},{3,15},{4,0},{5,1},{6,2},{7,3},{8,4},{9,5},{1... | collective-permute-start | bytes 307208 | tf_op jit(solution)/shard_map/ppermute | solution.py:165
  99.1 5.8 %collective-permute-start.11 = (s16[16,3200]{1,0:T(8,128)(2,1)S(1)}, s16[16,3200]{1,0:T(8,128)(2,1)S(1)}, u32[]{:S(2)}, u32[]{:S(2)}) collective-permute-start(s16[16,3200]{1,0:T(8,128)(2,1)S(1)} %get-tuple-element.25), channel_id=1, source_target_pairs={{0,4},{1,5},{2,6},{3,7},{4,8},{5,9},{6,10},{7,11},{8,12},{9,13},{1... | collective-permute-start | bytes 307208 | tf_op jit(solution)/shard_map/ppermute | solution.py:165
  101.0 11.3 %copy-start.7 = (f32[1600]{0:T(1024)S(1)}, f32[1600]{0:T(1024)}, u32[]{:S(2)}) copy-start(f32[1600]{0:T(1024)} %param.11) | copy-start | bytes 19204
  101.0 11.3 %copy-start.9 = (s32[64]{0:T(128)S(1)}, s32[64]{0:T(128)}, u32[]{:S(2)}) copy-start(s32[64]{0:T(128)} %param.8) | copy-start | bytes 772
  101.0 11.3 %copy-start.10 = (s32[64]{0:T(128)S(1)}, s32[64]{0:T(128)}, u32[]{:S(2)}) copy-start(s32[64]{0:T(128)} %param.9) | copy-start | bytes 772
  105.5 9.0 %collective-permute-start.13 = (f32[64,384]{1,0:T(8,128)S(1)}, f32[64,384]{1,0:T(8,128)S(1)}, u32[]{:S(2)}, u32[]{:S(2)}) collective-permute-start(f32[64,384]{1,0:T(8,128)S(1)} %get-tuple-element.48), channel_id=1, source_target_pairs={{0,0},{1,16},{2,2},{3,18},{4,4},{5,20},{6,6},{7,22},{8,8},{9,24},{... | collective-permute-start | bytes 294920 | tf_op jit(solution)/shard_map/ppermute | solution.py:256
  112.2 2.6 %collective-permute-start.14 = (f32[64,384]{1,0:T(8,128)S(1)}, f32[64,384]{1,0:T(8,128)S(1)}, u32[]{:S(2)}, u32[]{:S(2)}) collective-permute-start(f32[64,384]{1,0:T(8,128)S(1)} %get-tuple-element.47), channel_id=1, source_target_pairs={{0,16},{1,0},{2,18},{3,2},{4,20},{5,4},{6,22},{7,6},{8,24},{9,8},{... | collective-permute-start | bytes 294920 | tf_op jit(solution)/shard_map/ppermute | solution.py:256

commit v4 on v3

--- a/solution.py
+++ b/solution.py
@@ -12,7 +12,7 @@
 SLICES = ((64, (0, 0, 0, 1, 1, 2, 4), "DUxxDxD", "xUDUDUU"),)
 UNITS = 32767.0
 SMALLEST = 2.0**-126
-LAST_DEPTH = 2048
+LAST_DEPTH = 5120
 DEPTH = 2048
 GROUPS = (((0, 4), (4, 6), (6, 8)),)
 ORDER = (
@@ -212,7 +212,7 @@
     one = coded_shape(n, width)
     pair = jax.ShapeDtypeStruct((2, *one), jnp.int16)
     outs = (jax.ShapeDtypeStruct((3, n, width), jnp.float32), pair, pair, jax.ShapeDtypeStruct(one, jnp.int16))
-    return multiply(kernel, blocks, own, other, earlier, outs, scratch, LAST_DEPTH, 18)
+    return multiply(kernel, blocks, own, other, earlier, outs, scratch, LAST_DEPTH, 28)
 
 
 def after(value, *others):

time: 117 us -> 116 us (level)
    unnamed x22 -> x24, local copies, waits for them, and re-layouts: 9.74 us -> 9.74 us
  transfers between devices with their start and end apart: 15 -> 15, of which waited for: 9 -> 9; matrix products, arithmetic and copies ran while one was open for 1% -> 1% of each run, Pallas kernels for 18% -> 19%
where the time goes in v4:
time: 116 us; the launch traced here: 115 us
  waiting for transfers between devices  51.9 us (45%)
  Pallas kernels  27.1 us (23%)
  starting transfers between devices  23 us (20%)
  local copies, waits for them, and re-layouts  9.76 us (8%)
  other arithmetic  2.48 us (2%)
    ppermute x7, waiting for transfers between devices, partials(): done[name] = lax.ppermute(block, 'row', row_perm((first[i], second[i])))  37.8 us
    pallas_call x3, Pallas kernels, multiply(): pl.pallas_call(kernel, grid=(depth // step,), in_specs=[pl.BlockSpec((n,...  21 us
    ppermute x5, waiting for transfers between devices, along_z(): return lax.ppermute(sums, 'col', pairs)  11.9 us
    unnamed x24, local copies, waits for them, and re-layouts  9.74 us
    ppermute x5, starting transfers between devices, along_z(): return lax.ppermute(sums, 'col', pairs)  7.57 us
    ppermute x1, starting transfers between devices, on_device(): lax.ppermute(jnp.where(same, own, theirs), ('row', 'col'), swap_perm(0))  6.78 us
    pallas_call x2, Pallas kernels, turned(): pl.pallas_call(turn_kernel, grid=(depth // DEPTH,), in_specs=[pl.BlockSpe...  5.76 us
    ppermute x7, starting transfers between devices, partials(): done[name] = lax.ppermute(block, 'row', row_perm((first[i], second[i])))  5.36 us
  transfers between devices with their start and end apart: 15, of which 9 were waited for; matrix products, arithmetic and copies ran while one was open for 1% of the time, Pallas kernels for 19%

profile of v4, /device:TPU:1, one launch (start us, length us, event | category | flops | bytes accessed | tf_op | source)
XLA Modules:
  0.0 114.6 jit_solution(15167482494733822848)
XLA Ops:
  0.0 3.2 %collective-permute-start.5 = (bf16[384,10240]{1,0:T(8,128)(2,1)}, bf16[384,10240]{1,0:T(8,128)(2,1)S(1)}, u32[]{:S(2)}, u32[]{:S(2)}) collective-permute-start(bf16[384,10240]{1,0:T(8,128)(2,1)} %rows.1), channel_id=1, source_target_pairs={{0,16},{16,0},{32,48},{48,32},{64,80},{80,64},{96,112},{112,96},{1... | collective-permute-start | bytes 23592968 | tf_op jit(solution)/shard_map/ppermute | solution.py:223
  3.2 0.0 collective-permute-start.2
  3.2 0.8 collective-permute-start
  4.0 1.9 %collective-permute-start.6 = (bf16[64,10240]{1,0:T(8,128)(2,1)}, bf16[64,10240]{1,0:T(8,128)(2,1)S(1)}, u32[]{:S(2)}, u32[]{:S(2)}) collective-permute-start(bf16[64,10240]{1,0:T(8,128)(2,1)} %bitcast.11), channel_id=1, source_target_pairs={{0,128},{16,112},{32,160},{48,16},{64,192},{80,48},{96,224},{112,8... | collective-permute-start | bytes 3932168 | tf_op jit(solution)/shard_map/ppermute | solution.py:234
  5.9 3.2 %copy-done.6 = bf16[384,10240]{1,0:T(8,128)(2,1)S(1)} copy-done((bf16[384,10240]{1,0:T(8,128)(2,1)S(1)}, bf16[384,10240]{1,0:T(8,128)(2,1)}, u32[]{:S(2)}) %copy-start.6) | copy-done | bytes 7864344
  9.2 2.9 %shard_map.64.refs_2_.refs_4_ = bf16[10240,384]{1,0:T(8,128)(2,1)S(1)} custom-call(bf16[384,10240]{1,0:T(8,128)(2,1)S(1)} %copy-done.6), custom_call_target="tpu_custom_call" | custom-call | tf_op jit(solution)/shard_map/pallas_call | solution.py:65
  12.0 0.0 copy-start
  12.0 0.0 copy-start.7
  12.1 19.7 %collective-permute-done.2.refs_1_ = bf16[64,10240]{1,0:T(8,128)(2,1)} collective-permute-done((bf16[64,10240]{1,0:T(8,128)(2,1)}, bf16[64,10240]{1,0:T(8,128)(2,1)}, u32[]{:S(2)}, u32[]{:S(2)}) %collective-permute-start.2) | collective-permute-done | bytes 1310752 | tf_op jit(solution)/shard_map/ppermute | solution.py:234
  31.8 0.0 collective-permute-start.3
  31.8 2.7 %collective-permute-start.4 = (bf16[64,10240]{1,0:T(8,128)(2,1)}, bf16[64,10240]{1,0:T(8,128)(2,1)}, u32[]{:S(2)}, u32[]{:S(2)}) collective-permute-start(bf16[64,10240]{1,0:T(8,128)(2,1)} %collective-permute-done.2.refs_1_), channel_id=1, source_target_pairs={{0,96},{16,112},{32,0},{48,16},{64,32},{80,48},{96,64},{112,80},{1... | collective-permute-start | bytes 3932168 | tf_op jit(solution)/shard_map/ppermute | solution.py:234
  34.5 0.0 collective-permute-done.refs_2_
  34.5 0.0 collective-permute-start.1
  34.5 0.0 collective-permute-done.5.rows
  34.5 2.9 %shard_map.65.refs_3_.refs_5_ = bf16[10240,384]{1,0:T(8,128)(2,1)S(1)} custom-call(bf16[384,10240]{1,0:T(8,128)(2,1)S(1)} %collective-permute-done.5.rows), custom_call_target="tpu_custom_call" | custom-call | tf_op jit(solution)/shard_map/pallas_call | solution.py:65
  37.4 0.0 copy-start.3
  37.4 0.0 collective-permute-done.6.refs_3_
  37.4 0.0 copy-done
  37.4 0.0 copy-done.7
  37.4 9.2 %shard_map.67.refs_4_ = f32[256,768]{1,0:T(8,128)S(1)} custom-call(bf16[64,10240]{1,0:T(8,128)(2,1)S(1)} %bitcast.12, bf16[64,10240]{1,0:T(8,128)(2,1)} %collective-permute-done.2.refs_1_, bf16[64,10240]{1,0:T(8,128)(2,1)} %collective-permute-done.refs_2_, bf16[64,10240]{1,0:T(8,128)(2,1)S(1)} %collective-permute-done.6.refs_3_, ...), custom_call_target="tpu_custom_call" | custom-call | tf_op jit(solution)/shard_map/pallas_call | solution.py:187
  46.6 0.0 copy-done.3
  46.6 3.1 %collective-permute-done.3.refs_0_ = bf16[64,10240]{1,0:T(8,128)(2,1)S(1)} collective-permute-done((bf16[64,10240]{1,0:T(8,128)(2,1)}, bf16[64,10240]{1,0:T(8,128)(2,1)S(1)}, u32[]{:S(2)}, u32[]{:S(2)}) %collective-permute-start.3) | collective-permute-done | bytes 1310752 | tf_op jit(solution)/shard_map/ppermute | solution.py:234
  49.7 0.0 collective-permute-start.7
  49.7 10.3 %collective-permute-done.4.refs_1_ = bf16[64,10240]{1,0:T(8,128)(2,1)} collective-permute-done((bf16[64,10240]{1,0:T(8,128)(2,1)}, bf16[64,10240]{1,0:T(8,128)(2,1)}, u32[]{:S(2)}, u32[]{:S(2)}) %collective-permute-start.4) | collective-permute-done | bytes 1310752 | tf_op jit(solution)/shard_map/ppermute | solution.py:234
  60.0 3.2 %copy-done.1 = bf16[10240,384]{1,0:T(8,128)(2,1)S(1)} copy-done((bf16[10240,384]{1,0:T(8,128)(2,1)S(1)}, bf16[10240,384]{1,0:T(8,128)(2,1)}, u32[]{:S(2)}) %copy-start.1) | copy-done | bytes 7864344
  63.2 3.2 %copy-done.4 = bf16[10240,384]{1,0:T(8,128)(2,1)S(1)} copy-done((bf16[10240,384]{1,0:T(8,128)(2,1)S(1)}, bf16[10240,384]{1,0:T(8,128)(2,1)}, u32[]{:S(2)}) %copy-start.4) | copy-done | bytes 7864344
  66.4 6.7 %shard_map.66.refs_5_ = f32[128,768]{1,0:T(8,128)S(1)} custom-call(bf16[64,10240]{1,0:T(8,128)(2,1)S(1)} %collective-permute-done.3.refs_0_, bf16[64,10240]{1,0:T(8,128)(2,1)} %collective-permute-done.4.refs_1_, bf16[10240,384]{1,0:T(8,128)(2,1)S(1)} %copy-done.1, bf16[10240,384]{1,0:T(8,128)(2,1)S(1)} %copy-done.4), custom_call_target="tpu_custom_call" | custom-call | tf_op jit(solution)/shard_map/pallas_call | solution.py:187
  73.1 0.0 copy-start.9
  73.1 0.0 collective-permute-done.1.refs_0_
  73.1 4.7 %collective-permute-done.7.refs_1_ = bf16[64,10240]{1,0:T(8,128)(2,1)} collective-permute-done((bf16[64,10240]{1,0:T(8,128)(2,1)S(1)}, bf16[64,10240]{1,0:T(8,128)(2,1)}, u32[]{:S(2)}, u32[]{:S(2)}) %collective-permute-start.7) | collective-permute-done | bytes 1310752 | tf_op jit(solution)/shard_map/ppermute | solution.py:234
  77.9 0.0 copy-done.2
  77.9 0.0 copy-done.5
  77.9 5.2 %shard_map.68 = (f32[3,64,768]{2,1,0:T(8,128)S(1)}, s16[2,16,3200]{2,1,0:T(8,128)(2,1)S(1)}, s16[2,16,3200]{2,1,0:T(8,128)(2,1)S(1)}, s16[16,3200]{1,0:T(8,128)(2,1)S(1)}) custom-call(bf16[64,10240]{1,0:T(8,128)(2,1)S(1)} %collective-permute-done.1.refs_0_, bf16[64,10240]{1,0:T(8,128)(2,1)} %collective-permute-done.7.refs_1_, ...), custom_call_target="tpu_custom_call" | custom-call | tf_op jit(solution)/shard_map/pallas_call | solution.py:187
  83.1 1.0 collective-permute-start.8
  84.1 4.0 %collective-permute-start.9 = (s16[2,16,3200]{2,1,0:T(8,128)(2,1)S(1)}, s16[2,16,3200]{2,1,0:T(8,128)(2,1)S(1)}, u32[]{:S(2)}, u32[]{:S(2)}) collective-permute-start(s16[2,16,3200]{2,1,0:T(8,128)(2,1)S(1)} %get-tuple-element.23), channel_id=1, source_target_pairs={{0,14},{1,15},{2,0},{3,1},{4,2},{5,3},{6,4},{7,5},{8,6},{9,7},{10,... | collective-permute-start | bytes 614408 | tf_op jit(solution)/shard_map/ppermute | solution.py:165
  88.1 0.1 collective-permute-start.10
  88.2 0.0 copy-done.9
  88.2 0.2 select_reduce_fusion.2
  88.4 8.3 %collective-permute-done.10.from_far = s16[16,3200]{1,0:T(8,128)(2,1)S(1)} collective-permute-done((s16[16,3200]{1,0:T(8,128)(2,1)S(1)}, s16[16,3200]{1,0:T(8,128)(2,1)S(1)}, u32[]{:S(2)}, u32[]{:S(2)}) %collective-permute-start.10) | collective-permute-done | bytes 102432 | tf_op jit(solution)/shard_map/ppermute | solution.py:165
  96.7 0.0 collective-permute-done.8.from_below
  96.7 0.0 collective-permute-done.9.from_above
  96.7 0.3 shard_map.69
  97.1 1.2 %collective-permute-start.12 = (s16[16,3200]{1,0:T(8,128)(2,1)S(1)}, s16[16,3200]{1,0:T(8,128)(2,1)S(1)}, u32[]{:S(2)}, u32[]{:S(2)}) collective-permute-start(s16[16,3200]{1,0:T(8,128)(2,1)S(1)} %get-tuple-element.26), channel_id=1, source_target_pairs={{0,12},{1,13},{2,14},{3,15},{4,0},{5,1},{6,2},{7,3},{8,4},{9,5},{1... | collective-permute-start | bytes 307208 | tf_op jit(solution)/shard_map/ppermute | solution.py:165
  98.3 1.2 %collective-permute-start.11 = (s16[16,3200]{1,0:T(8,128)(2,1)S(1)}, s16[16,3200]{1,0:T(8,128)(2,1)S(1)}, u32[]{:S(2)}, u32[]{:S(2)}) collective-permute-start(s16[16,3200]{1,0:T(8,128)(2,1)S(1)} %get-tuple-element.25), channel_id=1, source_target_pairs={{0,4},{1,5},{2,6},{3,7},{4,8},{5,9},{6,10},{7,11},{8,12},{9,13},{1... | collective-permute-start | bytes 307208 | tf_op jit(solution)/shard_map/ppermute | solution.py:165
  99.5 0.2 fusion.39
  99.8 0.2 fusion.51
  100.0 0.1 convert_multiply_fusion.11
  100.1 0.0 copy-start.8
  100.1 0.0 copy-start.10
  100.1 0.0 copy-start.11
  100.1 0.1 convert_multiply_fusion.15
  100.2 1.8 %collective-permute-done.12 = s16[16,3200]{1,0:T(8,128)(2,1)S(1)} collective-permute-done((s16[16,3200]{1,0:T(8,128)(2,1)S(1)}, s16[16,3200]{1,0:T(8,128)(2,1)S(1)}, u32[]{:S(2)}, u32[]{:S(2)}) %collective-permute-start.12) | collective-permute-done | bytes 102432 | tf_op jit(solution)/shard_map/ppermute | solution.py:165
  102.0 0.2 fusion.15
  102.2 1.8 %collective-permute-done.11 = s16[16,3200]{1,0:T(8,128)(2,1)S(1)} collective-permute-done((s16[16,3200]{1,0:T(8,128)(2,1)S(1)}, s16[16,3200]{1,0:T(8,128)(2,1)S(1)}, u32[]{:S(2)}, u32[]{:S(2)}) %collective-permute-start.11) | collective-permute-done | bytes 102432 | tf_op jit(solution)/shard_map/ppermute | solution.py:165
  104.0 0.2 fusion.27
  104.3 0.1 convert_multiply_fusion.3
  104.4 0.1 convert_multiply_fusion.7
  104.4 0.1 fusion.2
  104.5 6.8 %collective-permute-start.13 = (f32[64,384]{1,0:T(8,128)S(1)}, f32[64,384]{1,0:T(8,128)S(1)}, u32[]{:S(2)}, u32[]{:S(2)}) collective-permute-start(f32[64,384]{1,0:T(8,128)S(1)} %get-tuple-element.48), channel_id=1, source_target_pairs={{0,0},{1,16},{2,2},{3,18},{4,4},{5,20},{6,6},{7,22},{8,8},{9,24},{... | collective-permute-start | bytes 294920 | tf_op jit(solution)/shard_map/ppermute | solution.py:256
  111.3 0.1 collective-permute-start.14
  111.5 0.3 select_reduce_fusion.1
  111.7 1.9 %collective-permute-done.13 = f32[64,384]{1,0:T(8,128)S(1)} collective-permute-done((f32[64,384]{1,0:T(8,128)S(1)}, f32[64,384]{1,0:T(8,128)S(1)}, u32[]{:S(2)}, u32[]{:S(2)}) %collective-permute-start.13) | collective-permute-done | bytes 98336 | tf_op jit(solution)/shard_map/ppermute | solution.py:256
  113.6 0.3 collective-permute-done.14
  113.9 0.7 fusion.3
  (17 shorter events, 0.1 us)
Async XLA Ops:
  0.0 34.5 %collective-permute-start.5 = (bf16[384,10240]{1,0:T(8,128)(2,1)}, bf16[384,10240]{1,0:T(8,128)(2,1)S(1)}, u32[]{:S(2)}, u32[]{:S(2)}) collective-permute-start(bf16[384,10240]{1,0:T(8,128)(2,1)} %rows.1), channel_id=1, source_target_pairs={{0,16},{16,0},{32,48},{48,32},{64,80},{80,64},{96,112},{112,96},{1... | collective-permute-start | bytes 23592968 | tf_op jit(solution)/shard_map/ppermute | solution.py:223
  3.2 28.6 %collective-permute-start.2 = (bf16[64,10240]{1,0:T(8,128)(2,1)}, bf16[64,10240]{1,0:T(8,128)(2,1)}, u32[]{:S(2)}, u32[]{:S(2)}) collective-permute-start(bf16[64,10240]{1,0:T(8,128)(2,1)} %bitcast.9), channel_id=1, source_target_pairs={{0,96},{16,144},{32,0},{48,176},{64,32},{80,208},{96,64},{112,240}... | collective-permute-start | bytes 3932168 | tf_op jit(solution)/shard_map/ppermute | solution.py:234
  3.2 31.2 %collective-permute-start = (bf16[64,10240]{1,0:T(8,128)(2,1)}, bf16[64,10240]{1,0:T(8,128)(2,1)}, u32[]{:S(2)}, u32[]{:S(2)}) collective-permute-start(bf16[64,10240]{1,0:T(8,128)(2,1)} %bitcast.10), channel_id=1, source_target_pairs={{0,32},{16,48},{32,64},{48,80},{64,96},{80,112},{96,0},{112,16},{1... | collective-permute-start | bytes 3932168 | tf_op jit(solution)/shard_map/ppermute | solution.py:234
  4.0 33.4 %collective-permute-start.6 = (bf16[64,10240]{1,0:T(8,128)(2,1)}, bf16[64,10240]{1,0:T(8,128)(2,1)S(1)}, u32[]{:S(2)}, u32[]{:S(2)}) collective-permute-start(bf16[64,10240]{1,0:T(8,128)(2,1)} %bitcast.11), channel_id=1, source_target_pairs={{0,128},{16,112},{32,160},{48,16},{64,192},{80,48},{96,224},{112,8... | collective-permute-start | bytes 3932168 | tf_op jit(solution)/shard_map/ppermute | solution.py:234
  5.9 3.2 %copy-start.6 = (bf16[384,10240]{1,0:T(8,128)(2,1)S(1)}, bf16[384,10240]{1,0:T(8,128)(2,1)}, u32[]{:S(2)}) copy-start(bf16[384,10240]{1,0:T(8,128)(2,1)} %rows.1) | copy-start | bytes 23592964
  12.0 25.4 %copy-start = (bf16[10240,384]{1,0:T(8,128)(2,1)}, bf16[10240,384]{1,0:T(8,128)(2,1)S(1)}, u32[]{:S(2)}) copy-start(bf16[10240,384]{1,0:T(8,128)(2,1)S(1)} %shard_map.64.refs_2_.refs_4_) | copy-start | bytes 23592964
  12.0 25.4 %copy-start.7 = (bf16[10240,64]{0,1:T(8,128)(2,1)S(1)}, bf16[10240,64]{0,1:T(8,128)(2,1)}, u32[]{:S(2)}) copy-start(bf16[10240,64]{0,1:T(8,128)(2,1)} %param.7) | copy-start | bytes 3932164
  31.8 17.9 %collective-permute-start.3 = (bf16[64,10240]{1,0:T(8,128)(2,1)}, bf16[64,10240]{1,0:T(8,128)(2,1)S(1)}, u32[]{:S(2)}, u32[]{:S(2)}) collective-permute-start(bf16[64,10240]{1,0:T(8,128)(2,1)} %collective-permute-done.2.refs_1_), channel_id=1, source_target_pairs={{0,128},{16,48},{32,160},{48,80},{64,192},{80,112},{96,224},{112,1... | collective-permute-start | bytes 3932168 | tf_op jit(solution)/shard_map/ppermute | solution.py:234
  31.8 28.2 %collective-permute-start.4 = (bf16[64,10240]{1,0:T(8,128)(2,1)}, bf16[64,10240]{1,0:T(8,128)(2,1)}, u32[]{:S(2)}, u32[]{:S(2)}) collective-permute-start(bf16[64,10240]{1,0:T(8,128)(2,1)} %collective-permute-done.2.refs_1_), channel_id=1, source_target_pairs={{0,96},{16,112},{32,0},{48,16},{64,32},{80,48},{96,64},{112,80},{1... | collective-permute-start | bytes 3932168 | tf_op jit(solution)/shard_map/ppermute | solution.py:234
  34.5 38.7 %collective-permute-start.1 = (bf16[64,10240]{1,0:T(8,128)(2,1)}, bf16[64,10240]{1,0:T(8,128)(2,1)S(1)}, u32[]{:S(2)}, u32[]{:S(2)}) collective-permute-start(bf16[64,10240]{1,0:T(8,128)(2,1)} %collective-permute-done.refs_2_), channel_id=1, source_target_pairs={{0,128},{16,48},{32,160},{48,80},{64,192},{80,112},{96,224},{112,1... | collective-permute-start | bytes 3932168 | tf_op jit(solution)/shard_map/ppermute | solution.py:234
  37.4 9.2 %copy-start.3 = (bf16[10240,384]{1,0:T(8,128)(2,1)}, bf16[10240,384]{1,0:T(8,128)(2,1)S(1)}, u32[]{:S(2)}) copy-start(bf16[10240,384]{1,0:T(8,128)(2,1)S(1)} %shard_map.65.refs_3_.refs_5_) | copy-start | bytes 23592964
  49.7 28.2 %collective-permute-start.7 = (bf16[64,10240]{1,0:T(8,128)(2,1)S(1)}, bf16[64,10240]{1,0:T(8,128)(2,1)}, u32[]{:S(2)}, u32[]{:S(2)}) collective-permute-start(bf16[64,10240]{1,0:T(8,128)(2,1)S(1)} %collective-permute-done.3.refs_0_), channel_id=1, source_target_pairs={{0,96},{16,48},{32,0},{48,80},{64,32},{80,112},{96,64},{112,16},{1... | collective-permute-start | bytes 3932168 | tf_op jit(solution)/shard_map/ppermute | solution.py:234
  60.0 3.2 %copy-start.1 = (bf16[10240,384]{1,0:T(8,128)(2,1)S(1)}, bf16[10240,384]{1,0:T(8,128)(2,1)}, u32[]{:S(2)}) copy-start(bf16[10240,384]{1,0:T(8,128)(2,1)} %copy-done) | copy-start | bytes 23592964
  63.2 3.2 %copy-start.4 = (bf16[10240,384]{1,0:T(8,128)(2,1)S(1)}, bf16[10240,384]{1,0:T(8,128)(2,1)}, u32[]{:S(2)}) copy-start(bf16[10240,384]{1,0:T(8,128)(2,1)} %copy-done.3) | copy-start | bytes 23592964
  66.4 11.4 %copy-start.2 = (bf16[10240,384]{1,0:T(8,128)(2,1)S(1)}, bf16[10240,384]{1,0:T(8,128)(2,1)}, u32[]{:S(2)}) copy-start(bf16[10240,384]{1,0:T(8,128)(2,1)} %copy-done) | copy-start | bytes 23592964
  66.4 11.4 %copy-start.5 = (bf16[10240,384]{1,0:T(8,128)(2,1)S(1)}, bf16[10240,384]{1,0:T(8,128)(2,1)}, u32[]{:S(2)}) copy-start(bf16[10240,384]{1,0:T(8,128)(2,1)} %copy-done.3) | copy-start | bytes 23592964
  73.1 15.1 %copy-start.9 = (f32[200]{0:T(256)S(1)}, f32[200]{0:T(256)}, u32[]{:S(2)}) copy-start(f32[200]{0:T(256)} %param.10) | copy-start | bytes 2404
  83.1 13.7 %collective-permute-start.8 = (s16[2,16,3200]{2,1,0:T(8,128)(2,1)S(1)}, s16[2,16,3200]{2,1,0:T(8,128)(2,1)S(1)}, u32[]{:S(2)}, u32[]{:S(2)}) collective-permute-start(s16[2,16,3200]{2,1,0:T(8,128)(2,1)S(1)} %get-tuple-element.22), channel_id=1, source_target_pairs={{0,2},{1,3},{2,4},{3,5},{4,6},{5,7},{6,8},{7,9},{8,10},{9,11},{10,... | collective-permute-start | bytes 614408 | tf_op jit(solution)/shard_map/ppermute | solution.py:165
  84.1 12.6 %collective-permute-start.9 = (s16[2,16,3200]{2,1,0:T(8,128)(2,1)S(1)}, s16[2,16,3200]{2,1,0:T(8,128)(2,1)S(1)}, u32[]{:S(2)}, u32[]{:S(2)}) collective-permute-start(s16[2,16,3200]{2,1,0:T(8,128)(2,1)S(1)} %get-tuple-element.23), channel_id=1, source_target_pairs={{0,14},{1,15},{2,0},{3,1},{4,2},{5,3},{6,4},{7,5},{8,6},{9,7},{10,... | collective-permute-start | bytes 614408 | tf_op jit(solution)/shard_map/ppermute | solution.py:165
  88.1 8.6 %collective-permute-start.10 = (s16[16,3200]{1,0:T(8,128)(2,1)S(1)}, s16[16,3200]{1,0:T(8,128)(2,1)S(1)}, u32[]{:S(2)}, u32[]{:S(2)}) collective-permute-start(s16[16,3200]{1,0:T(8,128)(2,1)S(1)} %get-tuple-element.24), channel_id=1, source_target_pairs={{0,4},{1,5},{2,14},{3,15},{4,8},{5,9},{6,2},{7,3},{8,12},{9,13},{1... | collective-permute-start | bytes 307208 | tf_op jit(solution)/shard_map/ppermute | solution.py:165
  97.1 4.9 %collective-permute-start.12 = (s16[16,3200]{1,0:T(8,128)(2,1)S(1)}, s16[16,3200]{1,0:T(8,128)(2,1)S(1)}, u32[]{:S(2)}, u32[]{:S(2)}) collective-permute-start(s16[16,3200]{1,0:T(8,128)(2,1)S(1)} %get-tuple-element.26), channel_id=1, source_target_pairs={{0,12},{1,13},{2,14},{3,15},{4,0},{5,1},{6,2},{7,3},{8,4},{9,5},{1... | collective-permute-start | bytes 307208 | tf_op jit(solution)/shard_map/ppermute | solution.py:165
  98.3 5.7 %collective-permute-start.11 = (s16[16,3200]{1,0:T(8,128)(2,1)S(1)}, s16[16,3200]{1,0:T(8,128)(2,1)S(1)}, u32[]{:S(2)}, u32[]{:S(2)}) collective-permute-start(s16[16,3200]{1,0:T(8,128)(2,1)S(1)} %get-tuple-element.25), channel_id=1, source_target_pairs={{0,4},{1,5},{2,6},{3,7},{4,8},{5,9},{6,10},{7,11},{8,12},{9,13},{1... | collective-permute-start | bytes 307208 | tf_op jit(solution)/shard_map/ppermute | solution.py:165
  100.1 11.3 %copy-start.8 = (f32[1600]{0:T(1024)S(1)}, f32[1600]{0:T(1024)}, u32[]{:S(2)}) copy-start(f32[1600]{0:T(1024)} %param.11) | copy-start | bytes 19204
  100.1 11.3 %copy-start.10 = (s32[64]{0:T(128)S(1)}, s32[64]{0:T(128)}, u32[]{:S(2)}) copy-start(s32[64]{0:T(128)} %param.8) | copy-start | bytes 772
  100.1 11.3 %copy-start.11 = (s32[64]{0:T(128)S(1)}, s32[64]{0:T(128)}, u32[]{:S(2)}) copy-start(s32[64]{0:T(128)} %param.9) | copy-start | bytes 772
  104.5 9.1 %collective-permute-start.13 = (f32[64,384]{1,0:T(8,128)S(1)}, f32[64,384]{1,0:T(8,128)S(1)}, u32[]{:S(2)}, u32[]{:S(2)}) collective-permute-start(f32[64,384]{1,0:T(8,128)S(1)} %get-tuple-element.48), channel_id=1, source_target_pairs={{0,0},{1,16},{2,2},{3,18},{4,4},{5,20},{6,6},{7,22},{8,8},{9,24},{... | collective-permute-start | bytes 294920 | tf_op jit(solution)/shard_map/ppermute | solution.py:256
  111.3 2.6 %collective-permute-start.14 = (f32[64,384]{1,0:T(8,128)S(1)}, f32[64,384]{1,0:T(8,128)S(1)}, u32[]{:S(2)}, u32[]{:S(2)}) collective-permute-start(f32[64,384]{1,0:T(8,128)S(1)} %get-tuple-element.47), channel_id=1, source_target_pairs={{0,16},{1,0},{2,18},{3,2},{4,20},{5,4},{6,22},{7,6},{8,24},{9,8},{... | collective-permute-start | bytes 294920 | tf_op jit(solution)/shard_map/ppermute | solution.py:256

commit v5 on v4

--- a/solution.py
+++ b/solution.py
@@ -253,8 +253,8 @@
     same = h == core
     mine = sum_along_z(*partials(integrals.T, amplitudes))
     own, theirs = mine[:, :local_rows], mine[:, local_rows:]
-    ladder = lax.ppermute(jnp.where(same, own, theirs), ("row", "col"), swap_perm(0)) + lax.ppermute(
-        jnp.where(same, theirs, own), ("row", "col"), swap_perm(1)
+    ladder = lax.ppermute(jnp.where(same, theirs, own), ("row", "col"), swap_perm(1)) + lax.ppermute(
+        jnp.where(same, own, theirs), ("row", "col"), swap_perm(0)
     )
 
     nocc_count = occ_energy.shape[0]

time: 116 us -> 117 us (level)
  waiting for transfers between devices: 51.9 us -> 53.3 us
    ppermute x1, starting transfers between devices: 0.09 us -> 3.82 us  [on_device(): lax.ppermute(jnp.where(same, theirs, own), ('row', 'col'), swap_perm(1))]
    ppermute x1, starting transfers between devices: 6.78 us -> 3.58 us  [on_device(): lax.ppermute(jnp.where(same, own, theirs), ('row', 'col'), swap_perm(0))]
    ppermute x1, waiting for transfers between devices: 1.9 us -> 3.55 us  [on_device(): lax.ppermute(jnp.where(same, own, theirs), ('row', 'col'), swap_perm(0))]
  transfers between devices with their start and end apart: 15 -> 15, of which waited for: 9 -> 8; matrix products, arithmetic and copies ran while one was open for 1% -> 1% of each run, Pallas kernels for 19% -> 19%
where the time goes in v5:
time: 117 us; the launch traced here: 116 us
  waiting for transfers between devices  53.3 us (46%)
  Pallas kernels  27.1 us (23%)
  starting transfers between devices  23.6 us (20%)
  local copies, waits for them, and re-layouts  9.76 us (8%)
  other arithmetic  2.48 us (2%)
    ppermute x7, waiting for transfers between devices, partials(): done[name] = lax.ppermute(block, 'row', row_perm((first[i], second[i])))  37.8 us
    pallas_call x3, Pallas kernels, multiply(): pl.pallas_call(kernel, grid=(depth // step,), in_specs=[pl.BlockSpec((n,...  21 us
    ppermute x5, waiting for transfers between devices, along_z(): return lax.ppermute(sums, 'col', pairs)  11.9 us
    unnamed x24, local copies, waits for them, and re-layouts  9.74 us
    ppermute x5, starting transfers between devices, along_z(): return lax.ppermute(sums, 'col', pairs)  7.57 us
    pallas_call x2, Pallas kernels, turned(): pl.pallas_call(turn_kernel, grid=(depth // DEPTH,), in_specs=[pl.BlockSpe...  5.76 us
    ppermute x7, starting transfers between devices, partials(): done[name] = lax.ppermute(block, 'row', row_perm((first[i], second[i])))  5.36 us
    ppermute x1, starting transfers between devices, on_device(): lax.ppermute(jnp.where(same, theirs, own), ('row', 'col'), swap_perm(1))  3.82 us
  transfers between devices with their start and end apart: 15, of which 8 were waited for; matrix products, arithmetic and copies ran while one was open for 1% of the time, Pallas kernels for 19%

profile of v5, /device:TPU:1, one launch (start us, length us, event | category | flops | bytes accessed | tf_op | source)
XLA Modules:
  0.0 116.5 jit_solution(6397291610863778880)
XLA Ops:
  0.0 3.2 %collective-permute-start.5 = (bf16[384,10240]{1,0:T(8,128)(2,1)}, bf16[384,10240]{1,0:T(8,128)(2,1)S(1)}, u32[]{:S(2)}, u32[]{:S(2)}) collective-permute-start(bf16[384,10240]{1,0:T(8,128)(2,1)} %rows.1), channel_id=1, source_target_pairs={{0,16},{16,0},{32,48},{48,32},{64,80},{80,64},{96,112},{112,96},{1... | collective-permute-start | bytes 23592968 | tf_op jit(solution)/shard_map/ppermute | solution.py:223
  3.2 0.0 collective-permute-start.2
  3.2 0.8 collective-permute-start
  4.0 1.9 %collective-permute-start.6 = (bf16[64,10240]{1,0:T(8,128)(2,1)}, bf16[64,10240]{1,0:T(8,128)(2,1)S(1)}, u32[]{:S(2)}, u32[]{:S(2)}) collective-permute-start(bf16[64,10240]{1,0:T(8,128)(2,1)} %bitcast.11), channel_id=1, source_target_pairs={{0,128},{16,112},{32,160},{48,16},{64,192},{80,48},{96,224},{112,8... | collective-permute-start | bytes 3932168 | tf_op jit(solution)/shard_map/ppermute | solution.py:234
  5.9 3.2 %copy-done.6 = bf16[384,10240]{1,0:T(8,128)(2,1)S(1)} copy-done((bf16[384,10240]{1,0:T(8,128)(2,1)S(1)}, bf16[384,10240]{1,0:T(8,128)(2,1)}, u32[]{:S(2)}) %copy-start.6) | copy-done | bytes 7864344
  9.2 2.9 %shard_map.64.refs_2_.refs_4_ = bf16[10240,384]{1,0:T(8,128)(2,1)S(1)} custom-call(bf16[384,10240]{1,0:T(8,128)(2,1)S(1)} %copy-done.6), custom_call_target="tpu_custom_call" | custom-call | tf_op jit(solution)/shard_map/pallas_call | solution.py:65
  12.0 0.0 copy-start
  12.0 0.0 copy-start.7
  12.1 19.7 %collective-permute-done.2.refs_1_ = bf16[64,10240]{1,0:T(8,128)(2,1)} collective-permute-done((bf16[64,10240]{1,0:T(8,128)(2,1)}, bf16[64,10240]{1,0:T(8,128)(2,1)}, u32[]{:S(2)}, u32[]{:S(2)}) %collective-permute-start.2) | collective-permute-done | bytes 1310752 | tf_op jit(solution)/shard_map/ppermute | solution.py:234
  31.8 0.0 collective-permute-start.3
  31.8 2.7 %collective-permute-start.4 = (bf16[64,10240]{1,0:T(8,128)(2,1)}, bf16[64,10240]{1,0:T(8,128)(2,1)}, u32[]{:S(2)}, u32[]{:S(2)}) collective-permute-start(bf16[64,10240]{1,0:T(8,128)(2,1)} %collective-permute-done.2.refs_1_), channel_id=1, source_target_pairs={{0,96},{16,112},{32,0},{48,16},{64,32},{80,48},{96,64},{112,80},{1... | collective-permute-start | bytes 3932168 | tf_op jit(solution)/shard_map/ppermute | solution.py:234
  34.5 0.0 collective-permute-done.refs_2_
  34.5 0.0 collective-permute-start.1
  34.5 0.0 collective-permute-done.5.rows
  34.5 2.9 %shard_map.65.refs_3_.refs_5_ = bf16[10240,384]{1,0:T(8,128)(2,1)S(1)} custom-call(bf16[384,10240]{1,0:T(8,128)(2,1)S(1)} %collective-permute-done.5.rows), custom_call_target="tpu_custom_call" | custom-call | tf_op jit(solution)/shard_map/pallas_call | solution.py:65
  37.4 0.0 copy-start.3
  37.4 0.0 collective-permute-done.6.refs_3_
  37.4 0.0 copy-done
  37.4 0.0 copy-done.7
  37.4 9.2 %shard_map.67.refs_4_ = f32[256,768]{1,0:T(8,128)S(1)} custom-call(bf16[64,10240]{1,0:T(8,128)(2,1)S(1)} %bitcast.12, bf16[64,10240]{1,0:T(8,128)(2,1)} %collective-permute-done.2.refs_1_, bf16[64,10240]{1,0:T(8,128)(2,1)} %collective-permute-done.refs_2_, bf16[64,10240]{1,0:T(8,128)(2,1)S(1)} %collective-permute-done.6.refs_3_, ...), custom_call_target="tpu_custom_call" | custom-call | tf_op jit(solution)/shard_map/pallas_call | solution.py:187
  46.6 0.0 copy-done.3
  46.6 3.1 %collective-permute-done.3.refs_0_ = bf16[64,10240]{1,0:T(8,128)(2,1)S(1)} collective-permute-done((bf16[64,10240]{1,0:T(8,128)(2,1)}, bf16[64,10240]{1,0:T(8,128)(2,1)S(1)}, u32[]{:S(2)}, u32[]{:S(2)}) %collective-permute-start.3) | collective-permute-done | bytes 1310752 | tf_op jit(solution)/shard_map/ppermute | solution.py:234
  49.7 0.0 collective-permute-start.7
  49.7 10.3 %collective-permute-done.4.refs_1_ = bf16[64,10240]{1,0:T(8,128)(2,1)} collective-permute-done((bf16[64,10240]{1,0:T(8,128)(2,1)}, bf16[64,10240]{1,0:T(8,128)(2,1)}, u32[]{:S(2)}, u32[]{:S(2)}) %collective-permute-start.4) | collective-permute-done | bytes 1310752 | tf_op jit(solution)/shard_map/ppermute | solution.py:234
  60.0 3.2 %copy-done.1 = bf16[10240,384]{1,0:T(8,128)(2,1)S(1)} copy-done((bf16[10240,384]{1,0:T(8,128)(2,1)S(1)}, bf16[10240,384]{1,0:T(8,128)(2,1)}, u32[]{:S(2)}) %copy-start.1) | copy-done | bytes 7864344
  63.2 3.2 %copy-done.4 = bf16[10240,384]{1,0:T(8,128)(2,1)S(1)} copy-done((bf16[10240,384]{1,0:T(8,128)(2,1)S(1)}, bf16[10240,384]{1,0:T(8,128)(2,1)}, u32[]{:S(2)}) %copy-start.4) | copy-done | bytes 7864344
  66.4 6.7 %shard_map.66.refs_5_ = f32[128,768]{1,0:T(8,128)S(1)} custom-call(bf16[64,10240]{1,0:T(8,128)(2,1)S(1)} %collective-permute-done.3.refs_0_, bf16[64,10240]{1,0:T(8,128)(2,1)} %collective-permute-done.4.refs_1_, bf16[10240,384]{1,0:T(8,128)(2,1)S(1)} %copy-done.1, bf16[10240,384]{1,0:T(8,128)(2,1)S(1)} %copy-done.4), custom_call_target="tpu_custom_call" | custom-call | tf_op jit(solution)/shard_map/pallas_call | solution.py:187
  73.1 0.0 copy-start.9
  73.1 0.0 collective-permute-done.1.refs_0_
  73.1 4.7 %collective-permute-done.7.refs_1_ = bf16[64,10240]{1,0:T(8,128)(2,1)} collective-permute-done((bf16[64,10240]{1,0:T(8,128)(2,1)S(1)}, bf16[64,10240]{1,0:T(8,128)(2,1)}, u32[]{:S(2)}, u32[]{:S(2)}) %collective-permute-start.7) | collective-permute-done | bytes 1310752 | tf_op jit(solution)/shard_map/ppermute | solution.py:234
  77.9 0.0 copy-done.2
  77.9 0.0 copy-done.5
  77.9 5.2 %shard_map.68 = (f32[3,64,768]{2,1,0:T(8,128)S(1)}, s16[2,16,3200]{2,1,0:T(8,128)(2,1)S(1)}, s16[2,16,3200]{2,1,0:T(8,128)(2,1)S(1)}, s16[16,3200]{1,0:T(8,128)(2,1)S(1)}) custom-call(bf16[64,10240]{1,0:T(8,128)(2,1)S(1)} %collective-permute-done.1.refs_0_, bf16[64,10240]{1,0:T(8,128)(2,1)} %collective-permute-done.7.refs_1_, ...), custom_call_target="tpu_custom_call" | custom-call | tf_op jit(solution)/shard_map/pallas_call | solution.py:187
  83.1 1.0 collective-permute-start.8
  84.1 4.0 %collective-permute-start.9 = (s16[2,16,3200]{2,1,0:T(8,128)(2,1)S(1)}, s16[2,16,3200]{2,1,0:T(8,128)(2,1)S(1)}, u32[]{:S(2)}, u32[]{:S(2)}) collective-permute-start(s16[2,16,3200]{2,1,0:T(8,128)(2,1)S(1)} %get-tuple-element.23), channel_id=1, source_target_pairs={{0,14},{1,15},{2,0},{3,1},{4,2},{5,3},{6,4},{7,5},{8,6},{9,7},{10,... | collective-permute-start | bytes 614408 | tf_op jit(solution)/shard_map/ppermute | solution.py:165
  88.1 0.1 collective-permute-start.10
  88.2 0.0 copy-done.9
  88.2 0.2 select_reduce_fusion.2
  88.4 8.3 %collective-permute-done.10.from_far = s16[16,3200]{1,0:T(8,128)(2,1)S(1)} collective-permute-done((s16[16,3200]{1,0:T(8,128)(2,1)S(1)}, s16[16,3200]{1,0:T(8,128)(2,1)S(1)}, u32[]{:S(2)}, u32[]{:S(2)}) %collective-permute-start.10) | collective-permute-done | bytes 102432 | tf_op jit(solution)/shard_map/ppermute | solution.py:165
  96.7 0.0 collective-permute-done.8.from_below
  96.7 0.0 collective-permute-done.9.from_above
  96.7 0.3 shard_map.69
  97.1 1.2 %collective-permute-start.12 = (s16[16,3200]{1,0:T(8,128)(2,1)S(1)}, s16[16,3200]{1,0:T(8,128)(2,1)S(1)}, u32[]{:S(2)}, u32[]{:S(2)}) collective-permute-start(s16[16,3200]{1,0:T(8,128)(2,1)S(1)} %get-tuple-element.26), channel_id=1, source_target_pairs={{0,12},{1,13},{2,14},{3,15},{4,0},{5,1},{6,2},{7,3},{8,4},{9,5},{1... | collective-permute-start | bytes 307208 | tf_op jit(solution)/shard_map/ppermute | solution.py:165
  98.3 1.2 %collective-permute-start.11 = (s16[16,3200]{1,0:T(8,128)(2,1)S(1)}, s16[16,3200]{1,0:T(8,128)(2,1)S(1)}, u32[]{:S(2)}, u32[]{:S(2)}) collective-permute-start(s16[16,3200]{1,0:T(8,128)(2,1)S(1)} %get-tuple-element.25), channel_id=1, source_target_pairs={{0,4},{1,5},{2,6},{3,7},{4,8},{5,9},{6,10},{7,11},{8,12},{9,13},{1... | collective-permute-start | bytes 307208 | tf_op jit(solution)/shard_map/ppermute | solution.py:165
  99.5 0.2 fusion.39
  99.8 0.2 fusion.51
  100.0 0.1 convert_multiply_fusion.11
  100.1 0.0 copy-start.8
  100.1 0.0 copy-start.10
  100.1 0.0 copy-start.11
  100.1 0.1 convert_multiply_fusion.15
  100.2 1.8 %collective-permute-done.12 = s16[16,3200]{1,0:T(8,128)(2,1)S(1)} collective-permute-done((s16[16,3200]{1,0:T(8,128)(2,1)S(1)}, s16[16,3200]{1,0:T(8,128)(2,1)S(1)}, u32[]{:S(2)}, u32[]{:S(2)}) %collective-permute-start.12) | collective-permute-done | bytes 102432 | tf_op jit(solution)/shard_map/ppermute | solution.py:165
  102.0 0.2 fusion.15
  102.2 1.8 %collective-permute-done.11 = s16[16,3200]{1,0:T(8,128)(2,1)S(1)} collective-permute-done((s16[16,3200]{1,0:T(8,128)(2,1)S(1)}, s16[16,3200]{1,0:T(8,128)(2,1)S(1)}, u32[]{:S(2)}, u32[]{:S(2)}) %collective-permute-start.11) | collective-permute-done | bytes 102432 | tf_op jit(solution)/shard_map/ppermute | solution.py:165
  104.0 0.2 fusion.27
  104.3 0.1 convert_multiply_fusion.3
  104.4 0.1 convert_multiply_fusion.7
  104.4 0.1 fusion.2
  104.5 3.8 %collective-permute-start.13 = (f32[64,384]{1,0:T(8,128)S(1)}, f32[64,384]{1,0:T(8,128)S(1)}, u32[]{:S(2)}, u32[]{:S(2)}) collective-permute-start(f32[64,384]{1,0:T(8,128)S(1)} %get-tuple-element.48), channel_id=1, source_target_pairs={{0,16},{1,0},{2,18},{3,2},{4,20},{5,4},{6,22},{7,6},{8,24},{9,8},{... | collective-permute-start | bytes 294920 | tf_op jit(solution)/shard_map/ppermute | solution.py:256
  108.3 3.6 %collective-permute-start.14 = (f32[64,384]{1,0:T(8,128)S(1)}, f32[64,384]{1,0:T(8,128)S(1)}, u32[]{:S(2)}, u32[]{:S(2)}) collective-permute-start(f32[64,384]{1,0:T(8,128)S(1)} %get-tuple-element.47), channel_id=1, source_target_pairs={{0,0},{1,16},{2,2},{3,18},{4,4},{5,20},{6,6},{7,22},{8,8},{9,24},{... | collective-permute-start | bytes 294920 | tf_op jit(solution)/shard_map/ppermute | solution.py:256
  112.0 0.3 select_reduce_fusion.1
  112.2 0.0 collective-permute-done.13
  112.2 3.6 %collective-permute-done.14 = f32[64,384]{1,0:T(8,128)S(1)} collective-permute-done((f32[64,384]{1,0:T(8,128)S(1)}, f32[64,384]{1,0:T(8,128)S(1)}, u32[]{:S(2)}, u32[]{:S(2)}) %collective-permute-start.14) | collective-permute-done | bytes 98336 | tf_op jit(solution)/shard_map/ppermute | solution.py:256
  115.8 0.7 fusion.3
  (17 shorter events, 0.1 us)
Async XLA Ops:
  0.0 34.5 %collective-permute-start.5 = (bf16[384,10240]{1,0:T(8,128)(2,1)}, bf16[384,10240]{1,0:T(8,128)(2,1)S(1)}, u32[]{:S(2)}, u32[]{:S(2)}) collective-permute-start(bf16[384,10240]{1,0:T(8,128)(2,1)} %rows.1), channel_id=1, source_target_pairs={{0,16},{16,0},{32,48},{48,32},{64,80},{80,64},{96,112},{112,96},{1... | collective-permute-start | bytes 23592968 | tf_op jit(solution)/shard_map/ppermute | solution.py:223
  3.2 28.6 %collective-permute-start.2 = (bf16[64,10240]{1,0:T(8,128)(2,1)}, bf16[64,10240]{1,0:T(8,128)(2,1)}, u32[]{:S(2)}, u32[]{:S(2)}) collective-permute-start(bf16[64,10240]{1,0:T(8,128)(2,1)} %bitcast.9), channel_id=1, source_target_pairs={{0,96},{16,144},{32,0},{48,176},{64,32},{80,208},{96,64},{112,240}... | collective-permute-start | bytes 3932168 | tf_op jit(solution)/shard_map/ppermute | solution.py:234
  3.2 31.2 %collective-permute-start = (bf16[64,10240]{1,0:T(8,128)(2,1)}, bf16[64,10240]{1,0:T(8,128)(2,1)}, u32[]{:S(2)}, u32[]{:S(2)}) collective-permute-start(bf16[64,10240]{1,0:T(8,128)(2,1)} %bitcast.10), channel_id=1, source_target_pairs={{0,32},{16,48},{32,64},{48,80},{64,96},{80,112},{96,0},{112,16},{1... | collective-permute-start | bytes 3932168 | tf_op jit(solution)/shard_map/ppermute | solution.py:234
  4.0 33.4 %collective-permute-start.6 = (bf16[64,10240]{1,0:T(8,128)(2,1)}, bf16[64,10240]{1,0:T(8,128)(2,1)S(1)}, u32[]{:S(2)}, u32[]{:S(2)}) collective-permute-start(bf16[64,10240]{1,0:T(8,128)(2,1)} %bitcast.11), channel_id=1, source_target_pairs={{0,128},{16,112},{32,160},{48,16},{64,192},{80,48},{96,224},{112,8... | collective-permute-start | bytes 3932168 | tf_op jit(solution)/shard_map/ppermute | solution.py:234
  5.9 3.2 %copy-start.6 = (bf16[384,10240]{1,0:T(8,128)(2,1)S(1)}, bf16[384,10240]{1,0:T(8,128)(2,1)}, u32[]{:S(2)}) copy-start(bf16[384,10240]{1,0:T(8,128)(2,1)} %rows.1) | copy-start | bytes 23592964
  12.0 25.4 %copy-start = (bf16[10240,384]{1,0:T(8,128)(2,1)}, bf16[10240,384]{1,0:T(8,128)(2,1)S(1)}, u32[]{:S(2)}) copy-start(bf16[10240,384]{1,0:T(8,128)(2,1)S(1)} %shard_map.64.refs_2_.refs_4_) | copy-start | bytes 23592964
  12.0 25.4 %copy-start.7 = (bf16[10240,64]{0,1:T(8,128)(2,1)S(1)}, bf16[10240,64]{0,1:T(8,128)(2,1)}, u32[]{:S(2)}) copy-start(bf16[10240,64]{0,1:T(8,128)(2,1)} %param.7) | copy-start | bytes 3932164
  31.8 17.9 %collective-permute-start.3 = (bf16[64,10240]{1,0:T(8,128)(2,1)}, bf16[64,10240]{1,0:T(8,128)(2,1)S(1)}, u32[]{:S(2)}, u32[]{:S(2)}) collective-permute-start(bf16[64,10240]{1,0:T(8,128)(2,1)} %collective-permute-done.2.refs_1_), channel_id=1, source_target_pairs={{0,128},{16,48},{32,160},{48,80},{64,192},{80,112},{96,224},{112,1... | collective-permute-start | bytes 3932168 | tf_op jit(solution)/shard_map/ppermute | solution.py:234
  31.8 28.2 %collective-permute-start.4 = (bf16[64,10240]{1,0:T(8,128)(2,1)}, bf16[64,10240]{1,0:T(8,128)(2,1)}, u32[]{:S(2)}, u32[]{:S(2)}) collective-permute-start(bf16[64,10240]{1,0:T(8,128)(2,1)} %collective-permute-done.2.refs_1_), channel_id=1, source_target_pairs={{0,96},{16,112},{32,0},{48,16},{64,32},{80,48},{96,64},{112,80},{1... | collective-permute-start | bytes 3932168 | tf_op jit(solution)/shard_map/ppermute | solution.py:234
  34.5 38.7 %collective-permute-start.1 = (bf16[64,10240]{1,0:T(8,128)(2,1)}, bf16[64,10240]{1,0:T(8,128)(2,1)S(1)}, u32[]{:S(2)}, u32[]{:S(2)}) collective-permute-start(bf16[64,10240]{1,0:T(8,128)(2,1)} %collective-permute-done.refs_2_), channel_id=1, source_target_pairs={{0,128},{16,48},{32,160},{48,80},{64,192},{80,112},{96,224},{112,1... | collective-permute-start | bytes 3932168 | tf_op jit(solution)/shard_map/ppermute | solution.py:234
  37.4 9.2 %copy-start.3 = (bf16[10240,384]{1,0:T(8,128)(2,1)}, bf16[10240,384]{1,0:T(8,128)(2,1)S(1)}, u32[]{:S(2)}) copy-start(bf16[10240,384]{1,0:T(8,128)(2,1)S(1)} %shard_map.65.refs_3_.refs_5_) | copy-start | bytes 23592964
  49.7 28.2 %collective-permute-start.7 = (bf16[64,10240]{1,0:T(8,128)(2,1)S(1)}, bf16[64,10240]{1,0:T(8,128)(2,1)}, u32[]{:S(2)}, u32[]{:S(2)}) collective-permute-start(bf16[64,10240]{1,0:T(8,128)(2,1)S(1)} %collective-permute-done.3.refs_0_), channel_id=1, source_target_pairs={{0,96},{16,48},{32,0},{48,80},{64,32},{80,112},{96,64},{112,16},{1... | collective-permute-start | bytes 3932168 | tf_op jit(solution)/shard_map/ppermute | solution.py:234
  60.0 3.2 %copy-start.1 = (bf16[10240,384]{1,0:T(8,128)(2,1)S(1)}, bf16[10240,384]{1,0:T(8,128)(2,1)}, u32[]{:S(2)}) copy-start(bf16[10240,384]{1,0:T(8,128)(2,1)} %copy-done) | copy-start | bytes 23592964
  63.2 3.2 %copy-start.4 = (bf16[10240,384]{1,0:T(8,128)(2,1)S(1)}, bf16[10240,384]{1,0:T(8,128)(2,1)}, u32[]{:S(2)}) copy-start(bf16[10240,384]{1,0:T(8,128)(2,1)} %copy-done.3) | copy-start | bytes 23592964
  66.4 11.4 %copy-start.2 = (bf16[10240,384]{1,0:T(8,128)(2,1)S(1)}, bf16[10240,384]{1,0:T(8,128)(2,1)}, u32[]{:S(2)}) copy-start(bf16[10240,384]{1,0:T(8,128)(2,1)} %copy-done) | copy-start | bytes 23592964
  66.4 11.4 %copy-start.5 = (bf16[10240,384]{1,0:T(8,128)(2,1)S(1)}, bf16[10240,384]{1,0:T(8,128)(2,1)}, u32[]{:S(2)}) copy-start(bf16[10240,384]{1,0:T(8,128)(2,1)} %copy-done.3) | copy-start | bytes 23592964
  73.1 15.1 %copy-start.9 = (f32[200]{0:T(256)S(1)}, f32[200]{0:T(256)}, u32[]{:S(2)}) copy-start(f32[200]{0:T(256)} %param.10) | copy-start | bytes 2404
  83.1 13.7 %collective-permute-start.8 = (s16[2,16,3200]{2,1,0:T(8,128)(2,1)S(1)}, s16[2,16,3200]{2,1,0:T(8,128)(2,1)S(1)}, u32[]{:S(2)}, u32[]{:S(2)}) collective-permute-start(s16[2,16,3200]{2,1,0:T(8,128)(2,1)S(1)} %get-tuple-element.22), channel_id=1, source_target_pairs={{0,2},{1,3},{2,4},{3,5},{4,6},{5,7},{6,8},{7,9},{8,10},{9,11},{10,... | collective-permute-start | bytes 614408 | tf_op jit(solution)/shard_map/ppermute | solution.py:165
  84.1 12.6 %collective-permute-start.9 = (s16[2,16,3200]{2,1,0:T(8,128)(2,1)S(1)}, s16[2,16,3200]{2,1,0:T(8,128)(2,1)S(1)}, u32[]{:S(2)}, u32[]{:S(2)}) collective-permute-start(s16[2,16,3200]{2,1,0:T(8,128)(2,1)S(1)} %get-tuple-element.23), channel_id=1, source_target_pairs={{0,14},{1,15},{2,0},{3,1},{4,2},{5,3},{6,4},{7,5},{8,6},{9,7},{10,... | collective-permute-start | bytes 614408 | tf_op jit(solution)/shard_map/ppermute | solution.py:165
  88.1 8.6 %collective-permute-start.10 = (s16[16,3200]{1,0:T(8,128)(2,1)S(1)}, s16[16,3200]{1,0:T(8,128)(2,1)S(1)}, u32[]{:S(2)}, u32[]{:S(2)}) collective-permute-start(s16[16,3200]{1,0:T(8,128)(2,1)S(1)} %get-tuple-element.24), channel_id=1, source_target_pairs={{0,4},{1,5},{2,14},{3,15},{4,8},{5,9},{6,2},{7,3},{8,12},{9,13},{1... | collective-permute-start | bytes 307208 | tf_op jit(solution)/shard_map/ppermute | solution.py:165
  97.1 4.9 %collective-permute-start.12 = (s16[16,3200]{1,0:T(8,128)(2,1)S(1)}, s16[16,3200]{1,0:T(8,128)(2,1)S(1)}, u32[]{:S(2)}, u32[]{:S(2)}) collective-permute-start(s16[16,3200]{1,0:T(8,128)(2,1)S(1)} %get-tuple-element.26), channel_id=1, source_target_pairs={{0,12},{1,13},{2,14},{3,15},{4,0},{5,1},{6,2},{7,3},{8,4},{9,5},{1... | collective-permute-start | bytes 307208 | tf_op jit(solution)/shard_map/ppermute | solution.py:165
  98.3 5.7 %collective-permute-start.11 = (s16[16,3200]{1,0:T(8,128)(2,1)S(1)}, s16[16,3200]{1,0:T(8,128)(2,1)S(1)}, u32[]{:S(2)}, u32[]{:S(2)}) collective-permute-start(s16[16,3200]{1,0:T(8,128)(2,1)S(1)} %get-tuple-element.25), channel_id=1, source_target_pairs={{0,4},{1,5},{2,6},{3,7},{4,8},{5,9},{6,10},{7,11},{8,12},{9,13},{1... | collective-permute-start | bytes 307208 | tf_op jit(solution)/shard_map/ppermute | solution.py:165
  100.1 11.8 %copy-start.8 = (f32[1600]{0:T(1024)S(1)}, f32[1600]{0:T(1024)}, u32[]{:S(2)}) copy-start(f32[1600]{0:T(1024)} %param.11) | copy-start | bytes 19204
  100.1 11.8 %copy-start.10 = (s32[64]{0:T(128)S(1)}, s32[64]{0:T(128)}, u32[]{:S(2)}) copy-start(s32[64]{0:T(128)} %param.8) | copy-start | bytes 772
  100.1 11.8 %copy-start.11 = (s32[64]{0:T(128)S(1)}, s32[64]{0:T(128)}, u32[]{:S(2)}) copy-start(s32[64]{0:T(128)} %param.9) | copy-start | bytes 772
  104.5 7.7 %collective-permute-start.13 = (f32[64,384]{1,0:T(8,128)S(1)}, f32[64,384]{1,0:T(8,128)S(1)}, u32[]{:S(2)}, u32[]{:S(2)}) collective-permute-start(f32[64,384]{1,0:T(8,128)S(1)} %get-tuple-element.48), channel_id=1, source_target_pairs={{0,16},{1,0},{2,18},{3,2},{4,20},{5,4},{6,22},{7,6},{8,24},{9,8},{... | collective-permute-start | bytes 294920 | tf_op jit(solution)/shard_map/ppermute | solution.py:256
  108.3 7.4 %collective-permute-start.14 = (f32[64,384]{1,0:T(8,128)S(1)}, f32[64,384]{1,0:T(8,128)S(1)}, u32[]{:S(2)}, u32[]{:S(2)}) collective-permute-start(f32[64,384]{1,0:T(8,128)S(1)} %get-tuple-element.47), channel_id=1, source_target_pairs={{0,0},{1,16},{2,2},{3,18},{4,4},{5,20},{6,6},{7,22},{8,8},{9,24},{... | collective-permute-start | bytes 294920 | tf_op jit(solution)/shard_map/ppermute | solution.py:256
